TPU v7x, 256 devices: a whole 4x4x8 slice. The times are simulated.
256 devices in a mesh: blk: 256 (over y, x, z, core).
Axes of the slice: x: 4, y: 4, z: 8, core: 2. Of those that a mesh axis runs over, the one named last changes fastest.
Arguments:
- image_emb: bfloat16 [32768, 1152], P('blk'), may hold values from -0.59765625 to 0.59765625
- image_ids: int32 [32768], P('blk'), may hold values from 0 to 127
- text_feats: bfloat16 [32768, 1152], P('blk'), may hold values from -0.59765625 to 0.59765625
- text_ids: int32 [32768], P('blk'), may hold values from 0 to 127
- text_head: bfloat16 [1152, 1152], replicated, may hold values from -0.099609375 to 1.5
Outputs:
- grad_image: bfloat16 [32768, 1152], P('blk')
- grad_text: bfloat16 [32768, 1152], P('blk')
- grad_head: float32 [1152, 1152], replicated
All inputs are finite; a program needn't handle non-finite values.
Results may differ from a plain program's by a relative error of at most 0.0038.
The roundings to bfloat16 on the way count: a program that leaves them out, or rounds other values in their place, can miss the bound.
Values may be sent and summed in bfloat16 or wider, within the bound.
A program may use at most 64 MiB of HBM per device.

v0:
```python
import jax
import jax.numpy as jnp
from jax import lax
from jax.sharding import PartitionSpec as P

REACH = 6


def from_behind(value, axis, steps):
    count = lax.axis_size(axis)
    pairs = [(source, (source + steps) % count) for source in range(count)]
    return lax.ppermute(value, axis, pairs)


def pair_tile(image_z, image_ids, text_blk, text_idb):
    logit = (
        10.0
        * lax.dot_general(
            image_z, text_blk, (((1,), (1,)), ((), ())), preferred_element_type=jnp.float32
        )
        - 5.0
    )
    label = jnp.where(image_ids[:, None] == text_idb[None, :], 1.0, -1.0).astype(jnp.float32)
    coef = (-label * jax.nn.sigmoid(-label * logit)).astype(jnp.bfloat16)
    image_part = 10.0 * jnp.dot(coef, text_blk, preferred_element_type=jnp.float32)
    text_part = 10.0 * lax.dot_general(
        coef, image_z, (((0,), (0,)), ((), ())), preferred_element_type=jnp.float32
    )
    return (image_part, text_part)


def shards(image_emb, image_ids, text_feats, text_ids, text_head):
    pre = jnp.dot(text_feats, text_head, preferred_element_type=jnp.float32)
    text_inv = lax.rsqrt(jnp.sum(pre * pre, axis=-1, keepdims=True) + 1e-06)
    text_unit = pre * text_inv
    text_z = text_unit.astype(jnp.bfloat16)
    image_f = image_emb.astype(jnp.float32)
    image_inv = lax.rsqrt(jnp.sum(image_f * image_f, axis=-1, keepdims=True) + 1e-06)
    image_unit = image_f * image_inv
    image_z = image_unit.astype(jnp.bfloat16)
    reach = REACH
    empty_text = jnp.zeros(text_z.shape, jnp.float32)
    empty_image = jnp.zeros(image_z.shape, jnp.float32)
    start_z, start_id = from_behind((text_z, text_ids), "blk", -(reach - 1))

    def walk_step(step, carry):
        cur_z, cur_id, running, grad_iz = carry
        image_part, text_part = pair_tile(image_z, image_ids, cur_z, cur_id)
        next_z, next_id = from_behind((cur_z, cur_id), "blk", 1)
        moved = from_behind(running + text_part, "blk", 1)
        return (next_z, next_id, moved, grad_iz + image_part)

    cur_z, cur_id, running, grad_iz = lax.fori_loop(
        0, 2 * reach - 1, walk_step, (start_z, start_id, empty_text, empty_image)
    )
    image_part, text_part = pair_tile(image_z, image_ids, cur_z, cur_id)
    grad_iz = grad_iz + image_part
    grad_tz = from_behind(running + text_part, "blk", -reach)
    grad_image = (
        (grad_iz - image_unit * jnp.sum(image_unit * grad_iz, axis=-1, keepdims=True)) * image_inv
    ).astype(jnp.bfloat16)
    grad_pre = (
        (grad_tz - text_unit * jnp.sum(text_unit * grad_tz, axis=-1, keepdims=True)) * text_inv
    ).astype(jnp.bfloat16)
    grad_text = lax.dot_general(
        grad_pre, text_head, (((1,), (1,)), ((), ())), preferred_element_type=jnp.float32
    ).astype(jnp.bfloat16)
    head_term = lax.dot_general(
        text_feats, grad_pre, (((0,), (0,)), ((), ())), preferred_element_type=jnp.float32
    )
    grad_head = lax.psum(head_term, "blk")
    return (grad_image, grad_text, grad_head)


def solution(mesh):
    placed = (P("blk", None), P("blk"), P("blk", None), P("blk"), P())
    return jax.shard_map(
        shards,
        mesh=mesh,
        in_specs=placed,
        out_specs=(P("blk", None), P("blk", None), P()),
        check_vma=False,
    )
```

profile of v0, /device:TPU:1, one launch (start us, length us, event | category | flops | bytes accessed | tf_op | source)
XLA Modules:
  0.0 611.4 jit_solution(403670362434597077)
XLA Ops:
  7.2 12.1 %collective-permute-start.4 = (s32[128]{0:T(128)}, s32[128]{0:T(128)S(1)}, u32[]{:S(2)}, u32[]{:S(2)}) collective-permute-start(s32[128]{0:T(128)} %param.10), channel_id=1, source_target_pairs={{0,251},{1,252},{2,253},{3,254},{4,255},{5,0},{6,1},{7,2},{8,3},{9... | collective-permute-start | bytes 1544 | tf_op jit(solution)/shard_map/ppermute | solution.py:12
  24.6 16.1 %collective-permute-done.3 = bf16[128,1152]{1,0:T(8,128)(2,1)} collective-permute-done((bf16[128,1152]{1,0:T(8,128)(2,1)S(1)}, bf16[128,1152]{1,0:T(8,128)(2,1)}, u32[]{:S(2)}, u32[]{:S(2)}) %collective-permute-start.3) | collective-permute-done | bytes 294944 | tf_op jit(solution)/shard_map/ppermute | solution.py:12
  40.8 238.5 %while.19 = (s32[]{:T(128)}, bf16[128,1152]{1,0:T(8,128)(2,1)}, s32[128]{0:T(128)S(1)}, f32[128,1152]{1,0:T(8,128)S(1)}, f32[128,1152]{1,0:T(8,128)}, /*index=5*...) while((s32[]{:T(128)}, bf16[128,1152]{1,0:T(8,128)(2,1)}, s32[128]{0:T(128)S(1)}, ...), condition=%wide.region_3.4_spmd.clone, body=%wide.region_2.3_spmd.clone.sunk | while | flops 114163712 | bytes 7901435 | solution.py:53
  43.6 2.1 fusion.60
  48.6 7.5 %collective-permute-done.1 = s32[128]{0:T(128)S(1)} collective-permute-done((s32[128]{0:T(128)}, s32[128]{0:T(128)S(1)}, u32[]{:S(2)}, u32[]{:S(2)}) %collective-permute-start.1) | collective-permute-done | bytes 544 | tf_op jit(solution)/shard_map/while/body/eval_jaxpr/ppermute | solution.py:12
  58.9 2.1 fusion.60
  60.9 2.5 collective-permute-start.2
  64.4 2.2 fusion.61
  66.6 7.2 %collective-permute-done.1 = s32[128]{0:T(128)S(1)} collective-permute-done((s32[128]{0:T(128)}, s32[128]{0:T(128)S(1)}, u32[]{:S(2)}, u32[]{:S(2)}) %collective-permute-start.1) | collective-permute-done | bytes 544 | tf_op jit(solution)/shard_map/while/body/eval_jaxpr/ppermute | solution.py:12
  78.6 2.5 collective-permute-start.2
  82.0 2.2 fusion.61
  84.2 10.6 %collective-permute-done.1 = s32[128]{0:T(128)S(1)} collective-permute-done((s32[128]{0:T(128)}, s32[128]{0:T(128)S(1)}, u32[]{:S(2)}, u32[]{:S(2)}) %collective-permute-start.1) | collective-permute-done | bytes 544 | tf_op jit(solution)/shard_map/while/body/eval_jaxpr/ppermute | solution.py:12
  99.7 2.2 fusion.61
  101.9 15.9 %collective-permute-done.1 = s32[128]{0:T(128)S(1)} collective-permute-done((s32[128]{0:T(128)}, s32[128]{0:T(128)S(1)}, u32[]{:S(2)}, u32[]{:S(2)}) %collective-permute-start.1) | collective-permute-done | bytes 544 | tf_op jit(solution)/shard_map/while/body/eval_jaxpr/ppermute | solution.py:12
  122.8 2.2 fusion.61
  125.0 15.9 %collective-permute-done.1 = s32[128]{0:T(128)S(1)} collective-permute-done((s32[128]{0:T(128)}, s32[128]{0:T(128)S(1)}, u32[]{:S(2)}, u32[]{:S(2)}) %collective-permute-start.1) | collective-permute-done | bytes 544 | tf_op jit(solution)/shard_map/while/body/eval_jaxpr/ppermute | solution.py:12
  145.9 2.2 fusion.61
  148.0 15.9 %collective-permute-done.1 = s32[128]{0:T(128)S(1)} collective-permute-done((s32[128]{0:T(128)}, s32[128]{0:T(128)S(1)}, u32[]{:S(2)}, u32[]{:S(2)}) %collective-permute-start.1) | collective-permute-done | bytes 544 | tf_op jit(solution)/shard_map/while/body/eval_jaxpr/ppermute | solution.py:12
  168.9 2.2 fusion.61
  171.1 15.9 %collective-permute-done.1 = s32[128]{0:T(128)S(1)} collective-permute-done((s32[128]{0:T(128)}, s32[128]{0:T(128)S(1)}, u32[]{:S(2)}, u32[]{:S(2)}) %collective-permute-start.1) | collective-permute-done | bytes 544 | tf_op jit(solution)/shard_map/while/body/eval_jaxpr/ppermute | solution.py:12
  192.0 2.2 fusion.61
  194.2 15.9 %collective-permute-done.1 = s32[128]{0:T(128)S(1)} collective-permute-done((s32[128]{0:T(128)}, s32[128]{0:T(128)S(1)}, u32[]{:S(2)}, u32[]{:S(2)}) %collective-permute-start.1) | collective-permute-done | bytes 544 | tf_op jit(solution)/shard_map/while/body/eval_jaxpr/ppermute | solution.py:12
  215.1 2.2 fusion.61
  217.2 15.9 %collective-permute-done.1 = s32[128]{0:T(128)S(1)} collective-permute-done((s32[128]{0:T(128)}, s32[128]{0:T(128)S(1)}, u32[]{:S(2)}, u32[]{:S(2)}) %collective-permute-start.1) | collective-permute-done | bytes 544 | tf_op jit(solution)/shard_map/while/body/eval_jaxpr/ppermute | solution.py:12
  238.1 2.2 fusion.61
  240.3 15.9 %collective-permute-done.1 = s32[128]{0:T(128)S(1)} collective-permute-done((s32[128]{0:T(128)}, s32[128]{0:T(128)S(1)}, u32[]{:S(2)}, u32[]{:S(2)}) %collective-permute-start.1) | collective-permute-done | bytes 544 | tf_op jit(solution)/shard_map/while/body/eval_jaxpr/ppermute | solution.py:12
  261.2 2.2 fusion.61
  263.4 15.9 %collective-permute-done.1 = s32[128]{0:T(128)S(1)} collective-permute-done((s32[128]{0:T(128)}, s32[128]{0:T(128)S(1)}, u32[]{:S(2)}, u32[]{:S(2)}) %collective-permute-start.1) | collective-permute-done | bytes 544 | tf_op jit(solution)/shard_map/while/body/eval_jaxpr/ppermute | solution.py:12
  282.2 18.1 %collective-permute-done.5 = f32[128,1152]{1,0:T(8,128)S(1)} collective-permute-done((f32[128,1152]{1,0:T(8,128)S(1)}, f32[128,1152]{1,0:T(8,128)S(1)}, u32[]{:S(2)}, u32[]{:S(2)}) %collective-permute-start.5) | collective-permute-done | bytes 589856 | tf_op jit(solution)/shard_map/ppermute | solution.py:12
  301.4 3.3 convolution_bitcast_fusion
  308.8 288.9 %all-reduce.2.cloned.1.call-done = f32[1152,1152]{0,1:T(8,128)} async-done(((f32[1152,1152]{0,1:T(8,128)}), f32[1152,1152]{0,1:T(8,128)}) %all-reduce.2.cloned.1.call-update) | async-done | bytes 5308432 | tf_op jit(solution)/shard_map/psum | solution.py:71
  597.7 6.9 %copy.8 = f32[1152,1152]{1,0:T(8,128)} copy(f32[1152,1152]{0,1:T(8,128)} %all-reduce.2.cloned.1.call-done) | data formatting | bytes 10616832
  (162 shorter events, 67.9 us)
Async XLA Ops:
  7.2 590.5 %all-reduce.2.cloned.1.call-start = ((), (), s32[]{:S(2)}) async-start(), calls=%async_computation | async-start | bytes 10616832 | tf_op jit(solution)/shard_map/psum | solution.py:71
  7.2 17.4 %collective-permute-start.4 = (s32[128]{0:T(128)}, s32[128]{0:T(128)S(1)}, u32[]{:S(2)}, u32[]{:S(2)}) collective-permute-start(s32[128]{0:T(128)} %param.10), channel_id=1, source_target_pairs={{0,251},{1,252},{2,253},{3,254},{4,255},{5,0},{6,1},{7,2},{8,3},{9... | collective-permute-start | bytes 1544 | tf_op jit(solution)/shard_map/ppermute | solution.py:12
  22.0 18.7 %collective-permute-start.3 = (bf16[128,1152]{1,0:T(8,128)(2,1)S(1)}, bf16[128,1152]{1,0:T(8,128)(2,1)}, u32[]{:S(2)}, u32[]{:S(2)}) collective-permute-start(bf16[128,1152]{1,0:T(8,128)(2,1)S(1)} %multiply_convert_fusion.1), channel_id=1, source_target_pairs={{0,251},{1,252},{2,253},{3,254},{4,255},{5,0},{6,1},{7,2},{8,3},{9... | collective-permute-start | bytes 884744 | tf_op jit(solution)/shard_map/ppermute | solution.py:12
  60.9 12.8 %collective-permute-start.2 = (f32[128,1152]{1,0:T(8,128)}, f32[128,1152]{1,0:T(8,128)S(1)}, u32[]{:S(2)}, u32[]{:S(2)}) collective-permute-start(f32[128,1152]{1,0:T(8,128)} %fusion.60), channel_id=1, source_target_pairs={{0,1},{1,2},{2,3},{3,4},{4,5},{5,6},{6,7},{7,8},{8,9},{9,10},{10,1... | collective-permute-start | bytes 1769480 | tf_op jit(solution)/shard_map/while/body/eval_jaxpr/ppermute | solution.py:12
  78.6 16.2 %collective-permute-start.2 = (f32[128,1152]{1,0:T(8,128)}, f32[128,1152]{1,0:T(8,128)S(1)}, u32[]{:S(2)}, u32[]{:S(2)}) collective-permute-start(f32[128,1152]{1,0:T(8,128)} %fusion.60), channel_id=1, source_target_pairs={{0,1},{1,2},{2,3},{3,4},{4,5},{5,6},{6,7},{7,8},{8,9},{9,10},{10,1... | collective-permute-start | bytes 1769480 | tf_op jit(solution)/shard_map/while/body/eval_jaxpr/ppermute | solution.py:12
  81.1 13.7 %collective-permute-start = (bf16[128,1152]{1,0:T(8,128)(2,1)S(1)}, bf16[128,1152]{1,0:T(8,128)(2,1)}, u32[]{:S(2)}, u32[]{:S(2)}) collective-permute-start(bf16[128,1152]{1,0:T(8,128)(2,1)S(1)} %copy.15), channel_id=1, source_target_pairs={{0,1},{1,2},{2,3},{3,4},{4,5},{5,6},{6,7},{7,8},{8,9},{9,10},{10,1... | collective-permute-start | bytes 884744 | tf_op jit(solution)/shard_map/while/body/eval_jaxpr/ppermute | solution.py:12
  81.2 13.6 %collective-permute-start.1 = (s32[128]{0:T(128)}, s32[128]{0:T(128)S(1)}, u32[]{:S(2)}, u32[]{:S(2)}) collective-permute-start(s32[128]{0:T(128)} %copy.16), channel_id=1, source_target_pairs={{0,1},{1,2},{2,3},{3,4},{4,5},{5,6},{6,7},{7,8},{8,9},{9,10},{10,1... | collective-permute-start | bytes 1544 | tf_op jit(solution)/shard_map/while/body/eval_jaxpr/ppermute | solution.py:12
  99.6 18.2 %collective-permute-start.2 = (f32[128,1152]{1,0:T(8,128)}, f32[128,1152]{1,0:T(8,128)S(1)}, u32[]{:S(2)}, u32[]{:S(2)}) collective-permute-start(f32[128,1152]{1,0:T(8,128)} %fusion.60), channel_id=1, source_target_pairs={{0,1},{1,2},{2,3},{3,4},{4,5},{5,6},{6,7},{7,8},{8,9},{9,10},{10,1... | collective-permute-start | bytes 1769480 | tf_op jit(solution)/shard_map/while/body/eval_jaxpr/ppermute | solution.py:12
  99.6 18.2 %collective-permute-start = (bf16[128,1152]{1,0:T(8,128)(2,1)S(1)}, bf16[128,1152]{1,0:T(8,128)(2,1)}, u32[]{:S(2)}, u32[]{:S(2)}) collective-permute-start(bf16[128,1152]{1,0:T(8,128)(2,1)S(1)} %copy.15), channel_id=1, source_target_pairs={{0,1},{1,2},{2,3},{3,4},{4,5},{5,6},{6,7},{7,8},{8,9},{9,10},{10,1... | collective-permute-start | bytes 884744 | tf_op jit(solution)/shard_map/while/body/eval_jaxpr/ppermute | solution.py:12
  99.6 18.2 %collective-permute-start.1 = (s32[128]{0:T(128)}, s32[128]{0:T(128)S(1)}, u32[]{:S(2)}, u32[]{:S(2)}) collective-permute-start(s32[128]{0:T(128)} %copy.16), channel_id=1, source_target_pairs={{0,1},{1,2},{2,3},{3,4},{4,5},{5,6},{6,7},{7,8},{8,9},{9,10},{10,1... | collective-permute-start | bytes 1544 | tf_op jit(solution)/shard_map/while/body/eval_jaxpr/ppermute | solution.py:12
  122.7 18.2 %collective-permute-start.2 = (f32[128,1152]{1,0:T(8,128)}, f32[128,1152]{1,0:T(8,128)S(1)}, u32[]{:S(2)}, u32[]{:S(2)}) collective-permute-start(f32[128,1152]{1,0:T(8,128)} %fusion.60), channel_id=1, source_target_pairs={{0,1},{1,2},{2,3},{3,4},{4,5},{5,6},{6,7},{7,8},{8,9},{9,10},{10,1... | collective-permute-start | bytes 1769480 | tf_op jit(solution)/shard_map/while/body/eval_jaxpr/ppermute | solution.py:12
  122.7 18.2 %collective-permute-start = (bf16[128,1152]{1,0:T(8,128)(2,1)S(1)}, bf16[128,1152]{1,0:T(8,128)(2,1)}, u32[]{:S(2)}, u32[]{:S(2)}) collective-permute-start(bf16[128,1152]{1,0:T(8,128)(2,1)S(1)} %copy.15), channel_id=1, source_target_pairs={{0,1},{1,2},{2,3},{3,4},{4,5},{5,6},{6,7},{7,8},{8,9},{9,10},{10,1... | collective-permute-start | bytes 884744 | tf_op jit(solution)/shard_map/while/body/eval_jaxpr/ppermute | solution.py:12
  122.7 18.2 %collective-permute-start.1 = (s32[128]{0:T(128)}, s32[128]{0:T(128)S(1)}, u32[]{:S(2)}, u32[]{:S(2)}) collective-permute-start(s32[128]{0:T(128)} %copy.16), channel_id=1, source_target_pairs={{0,1},{1,2},{2,3},{3,4},{4,5},{5,6},{6,7},{7,8},{8,9},{9,10},{10,1... | collective-permute-start | bytes 1544 | tf_op jit(solution)/shard_map/while/body/eval_jaxpr/ppermute | solution.py:12
  145.8 18.2 %collective-permute-start.2 = (f32[128,1152]{1,0:T(8,128)}, f32[128,1152]{1,0:T(8,128)S(1)}, u32[]{:S(2)}, u32[]{:S(2)}) collective-permute-start(f32[128,1152]{1,0:T(8,128)} %fusion.60), channel_id=1, source_target_pairs={{0,1},{1,2},{2,3},{3,4},{4,5},{5,6},{6,7},{7,8},{8,9},{9,10},{10,1... | collective-permute-start | bytes 1769480 | tf_op jit(solution)/shard_map/while/body/eval_jaxpr/ppermute | solution.py:12
  145.8 18.2 %collective-permute-start = (bf16[128,1152]{1,0:T(8,128)(2,1)S(1)}, bf16[128,1152]{1,0:T(8,128)(2,1)}, u32[]{:S(2)}, u32[]{:S(2)}) collective-permute-start(bf16[128,1152]{1,0:T(8,128)(2,1)S(1)} %copy.15), channel_id=1, source_target_pairs={{0,1},{1,2},{2,3},{3,4},{4,5},{5,6},{6,7},{7,8},{8,9},{9,10},{10,1... | collective-permute-start | bytes 884744 | tf_op jit(solution)/shard_map/while/body/eval_jaxpr/ppermute | solution.py:12
  145.8 18.2 %collective-permute-start.1 = (s32[128]{0:T(128)}, s32[128]{0:T(128)S(1)}, u32[]{:S(2)}, u32[]{:S(2)}) collective-permute-start(s32[128]{0:T(128)} %copy.16), channel_id=1, source_target_pairs={{0,1},{1,2},{2,3},{3,4},{4,5},{5,6},{6,7},{7,8},{8,9},{9,10},{10,1... | collective-permute-start | bytes 1544 | tf_op jit(solution)/shard_map/while/body/eval_jaxpr/ppermute | solution.py:12
  168.8 18.2 %collective-permute-start.2 = (f32[128,1152]{1,0:T(8,128)}, f32[128,1152]{1,0:T(8,128)S(1)}, u32[]{:S(2)}, u32[]{:S(2)}) collective-permute-start(f32[128,1152]{1,0:T(8,128)} %fusion.60), channel_id=1, source_target_pairs={{0,1},{1,2},{2,3},{3,4},{4,5},{5,6},{6,7},{7,8},{8,9},{9,10},{10,1... | collective-permute-start | bytes 1769480 | tf_op jit(solution)/shard_map/while/body/eval_jaxpr/ppermute | solution.py:12
  168.8 18.2 %collective-permute-start = (bf16[128,1152]{1,0:T(8,128)(2,1)S(1)}, bf16[128,1152]{1,0:T(8,128)(2,1)}, u32[]{:S(2)}, u32[]{:S(2)}) collective-permute-start(bf16[128,1152]{1,0:T(8,128)(2,1)S(1)} %copy.15), channel_id=1, source_target_pairs={{0,1},{1,2},{2,3},{3,4},{4,5},{5,6},{6,7},{7,8},{8,9},{9,10},{10,1... | collective-permute-start | bytes 884744 | tf_op jit(solution)/shard_map/while/body/eval_jaxpr/ppermute | solution.py:12
  168.8 18.2 %collective-permute-start.1 = (s32[128]{0:T(128)}, s32[128]{0:T(128)S(1)}, u32[]{:S(2)}, u32[]{:S(2)}) collective-permute-start(s32[128]{0:T(128)} %copy.16), channel_id=1, source_target_pairs={{0,1},{1,2},{2,3},{3,4},{4,5},{5,6},{6,7},{7,8},{8,9},{9,10},{10,1... | collective-permute-start | bytes 1544 | tf_op jit(solution)/shard_map/while/body/eval_jaxpr/ppermute | solution.py:12
  191.9 18.2 %collective-permute-start.2 = (f32[128,1152]{1,0:T(8,128)}, f32[128,1152]{1,0:T(8,128)S(1)}, u32[]{:S(2)}, u32[]{:S(2)}) collective-permute-start(f32[128,1152]{1,0:T(8,128)} %fusion.60), channel_id=1, source_target_pairs={{0,1},{1,2},{2,3},{3,4},{4,5},{5,6},{6,7},{7,8},{8,9},{9,10},{10,1... | collective-permute-start | bytes 1769480 | tf_op jit(solution)/shard_map/while/body/eval_jaxpr/ppermute | solution.py:12
  191.9 18.2 %collective-permute-start = (bf16[128,1152]{1,0:T(8,128)(2,1)S(1)}, bf16[128,1152]{1,0:T(8,128)(2,1)}, u32[]{:S(2)}, u32[]{:S(2)}) collective-permute-start(bf16[128,1152]{1,0:T(8,128)(2,1)S(1)} %copy.15), channel_id=1, source_target_pairs={{0,1},{1,2},{2,3},{3,4},{4,5},{5,6},{6,7},{7,8},{8,9},{9,10},{10,1... | collective-permute-start | bytes 884744 | tf_op jit(solution)/shard_map/while/body/eval_jaxpr/ppermute | solution.py:12
  191.9 18.2 %collective-permute-start.1 = (s32[128]{0:T(128)}, s32[128]{0:T(128)S(1)}, u32[]{:S(2)}, u32[]{:S(2)}) collective-permute-start(s32[128]{0:T(128)} %copy.16), channel_id=1, source_target_pairs={{0,1},{1,2},{2,3},{3,4},{4,5},{5,6},{6,7},{7,8},{8,9},{9,10},{10,1... | collective-permute-start | bytes 1544 | tf_op jit(solution)/shard_map/while/body/eval_jaxpr/ppermute | solution.py:12
  215.0 18.2 %collective-permute-start.2 = (f32[128,1152]{1,0:T(8,128)}, f32[128,1152]{1,0:T(8,128)S(1)}, u32[]{:S(2)}, u32[]{:S(2)}) collective-permute-start(f32[128,1152]{1,0:T(8,128)} %fusion.60), channel_id=1, source_target_pairs={{0,1},{1,2},{2,3},{3,4},{4,5},{5,6},{6,7},{7,8},{8,9},{9,10},{10,1... | collective-permute-start | bytes 1769480 | tf_op jit(solution)/shard_map/while/body/eval_jaxpr/ppermute | solution.py:12
  215.0 18.2 %collective-permute-start = (bf16[128,1152]{1,0:T(8,128)(2,1)S(1)}, bf16[128,1152]{1,0:T(8,128)(2,1)}, u32[]{:S(2)}, u32[]{:S(2)}) collective-permute-start(bf16[128,1152]{1,0:T(8,128)(2,1)S(1)} %copy.15), channel_id=1, source_target_pairs={{0,1},{1,2},{2,3},{3,4},{4,5},{5,6},{6,7},{7,8},{8,9},{9,10},{10,1... | collective-permute-start | bytes 884744 | tf_op jit(solution)/shard_map/while/body/eval_jaxpr/ppermute | solution.py:12
  215.0 18.2 %collective-permute-start.1 = (s32[128]{0:T(128)}, s32[128]{0:T(128)S(1)}, u32[]{:S(2)}, u32[]{:S(2)}) collective-permute-start(s32[128]{0:T(128)} %copy.16), channel_id=1, source_target_pairs={{0,1},{1,2},{2,3},{3,4},{4,5},{5,6},{6,7},{7,8},{8,9},{9,10},{10,1... | collective-permute-start | bytes 1544 | tf_op jit(solution)/shard_map/while/body/eval_jaxpr/ppermute | solution.py:12
  238.0 18.2 %collective-permute-start.2 = (f32[128,1152]{1,0:T(8,128)}, f32[128,1152]{1,0:T(8,128)S(1)}, u32[]{:S(2)}, u32[]{:S(2)}) collective-permute-start(f32[128,1152]{1,0:T(8,128)} %fusion.60), channel_id=1, source_target_pairs={{0,1},{1,2},{2,3},{3,4},{4,5},{5,6},{6,7},{7,8},{8,9},{9,10},{10,1... | collective-permute-start | bytes 1769480 | tf_op jit(solution)/shard_map/while/body/eval_jaxpr/ppermute | solution.py:12
  238.0 18.2 %collective-permute-start = (bf16[128,1152]{1,0:T(8,128)(2,1)S(1)}, bf16[128,1152]{1,0:T(8,128)(2,1)}, u32[]{:S(2)}, u32[]{:S(2)}) collective-permute-start(bf16[128,1152]{1,0:T(8,128)(2,1)S(1)} %copy.15), channel_id=1, source_target_pairs={{0,1},{1,2},{2,3},{3,4},{4,5},{5,6},{6,7},{7,8},{8,9},{9,10},{10,1... | collective-permute-start | bytes 884744 | tf_op jit(solution)/shard_map/while/body/eval_jaxpr/ppermute | solution.py:12
  238.0 18.2 %collective-permute-start.1 = (s32[128]{0:T(128)}, s32[128]{0:T(128)S(1)}, u32[]{:S(2)}, u32[]{:S(2)}) collective-permute-start(s32[128]{0:T(128)} %copy.16), channel_id=1, source_target_pairs={{0,1},{1,2},{2,3},{3,4},{4,5},{5,6},{6,7},{7,8},{8,9},{9,10},{10,1... | collective-permute-start | bytes 1544 | tf_op jit(solution)/shard_map/while/body/eval_jaxpr/ppermute | solution.py:12
  261.1 18.2 %collective-permute-start.2 = (f32[128,1152]{1,0:T(8,128)}, f32[128,1152]{1,0:T(8,128)S(1)}, u32[]{:S(2)}, u32[]{:S(2)}) collective-permute-start(f32[128,1152]{1,0:T(8,128)} %fusion.60), channel_id=1, source_target_pairs={{0,1},{1,2},{2,3},{3,4},{4,5},{5,6},{6,7},{7,8},{8,9},{9,10},{10,1... | collective-permute-start | bytes 1769480 | tf_op jit(solution)/shard_map/while/body/eval_jaxpr/ppermute | solution.py:12
  261.1 18.2 %collective-permute-start = (bf16[128,1152]{1,0:T(8,128)(2,1)S(1)}, bf16[128,1152]{1,0:T(8,128)(2,1)}, u32[]{:S(2)}, u32[]{:S(2)}) collective-permute-start(bf16[128,1152]{1,0:T(8,128)(2,1)S(1)} %copy.15), channel_id=1, source_target_pairs={{0,1},{1,2},{2,3},{3,4},{4,5},{5,6},{6,7},{7,8},{8,9},{9,10},{10,1... | collective-permute-start | bytes 884744 | tf_op jit(solution)/shard_map/while/body/eval_jaxpr/ppermute | solution.py:12
  261.1 18.2 %collective-permute-start.1 = (s32[128]{0:T(128)}, s32[128]{0:T(128)S(1)}, u32[]{:S(2)}, u32[]{:S(2)}) collective-permute-start(s32[128]{0:T(128)} %copy.16), channel_id=1, source_target_pairs={{0,1},{1,2},{2,3},{3,4},{4,5},{5,6},{6,7},{7,8},{8,9},{9,10},{10,1... | collective-permute-start | bytes 1544 | tf_op jit(solution)/shard_map/while/body/eval_jaxpr/ppermute | solution.py:12
  282.1 18.2 %collective-permute-start.5 = (f32[128,1152]{1,0:T(8,128)S(1)}, f32[128,1152]{1,0:T(8,128)S(1)}, u32[]{:S(2)}, u32[]{:S(2)}) collective-permute-start(f32[128,1152]{1,0:T(8,128)S(1)} %add.60), channel_id=1, source_target_pairs={{0,250},{1,251},{2,252},{3,253},{4,254},{5,255},{6,0},{7,1},{8,2},... | collective-permute-start | bytes 1769480 | tf_op jit(solution)/shard_map/ppermute | solution.py:12
  (27 other events, 186.1 us)
Sparse Core Ops, SparseCore 0:
  304.8 292.9 all-reduce.1
where the time goes:
time: 614 us; the launch traced here: 611 us
  waiting for transfers between devices  476 us (78%)
  matrix products  70.2 us (11%)
  local copies, waits for them, and re-layouts  25.4 us (4%)
  starting transfers between devices  22.7 us (4%)
  between operations  14.2 us (2%)
    psum x1, waiting for transfers between devices, shards(): grad_head = lax.psum(head_term, 'blk')  289 us
    ppermute x36, waiting for transfers between devices, from_behind(): return lax.ppermute(value, axis, pairs)  187 us
    dot_general x12, matrix products, pair_tile(): jnp.dot(coef, text_blk, preferred_element_type=jnp.float32)  24.8 us
    dot_general x12, matrix products, pair_tile(): lax.dot_general(coef, image_z, (((0,), (0,)), ((), ())), preferred_elemen...  23.9 us
    ppermute x36, starting transfers between devices, from_behind(): return lax.ppermute(value, axis, pairs)  22.6 us
    while x44, local copies, waits for them, and re-layouts  17 us
    dot_general x12, matrix products, pair_tile(): lax.dot_general(image_z, text_blk, (((1,), (1,)), ((), ())), preferred_el...  14.9 us
  transfers between devices with their start and end apart: 37, of which 14 were waited for; matrix products, arithmetic and copies ran while one was open for 5% of the time, Pallas kernels for 0%

commit v1 on v0

v1 whole, which is shorter than its diff:
```python
import jax
import jax.numpy as jnp
from jax import lax
from jax.experimental import pallas as pl
from jax.experimental.pallas import tpu as pltpu
from jax.sharding import PartitionSpec as P

MESH = pl.DeviceIdType.MESH
D = 1152
B = 128
REACH = 6
SLICE = 80
XR = 96
OWNER = (0, 4, 8, 12, 2, 3, 7, 11, 15)
X_LANES = ((0, 384), (640, 256))
Y_LANES = ((384, 256), (896, 256))
NT = (((1,), (1,)), ((), ()))


def start_row(p):
    return pl.multiple_of(16 * ((9 * p) // 2), 16)


def kernel(
    img_ref, imgid_ref, txt_ref, txtid_ref, head_ref,
    gimg_ref, gtxt_ref, g_ref,
    imgs, txts, img_pair, txt_pair, ids, img_col, txt_col, acc_t, acc_i, got_t, got_i,
    pre, gp_t, feats, gp_in, part, sums, block,
    band_s, band_r, id_s, id_r, pair_s, pair_r, fa_s, fa_r, gp_s, gp_r, rs_s, rs_r, az_s, az_r,
    a2_s, a2_r, a3_s, a3_r, am_s, am_r,
):
    me = lax.axis_index("blk")
    core = lax.rem(me, 2)
    q = lax.rem(me, 16)
    z = q // 2
    p = me // 16
    x = lax.rem(p, 4)
    y = p // 4
    mate = me + 1 - 2 * core
    right, left = lax.rem(me + 2, 256), lax.rem(me + 254, 256)

    def at(y2, x2):
        return (y2 * 4 + x2) * 16 + q

    xp, xm = lax.rem(x + 1, 4), lax.rem(x + 3, 4)
    yp, ym = lax.rem(y + 1, 4), lax.rem(y + 3, 4)

    barrier = pltpu.get_barrier_semaphore()

    def greet(device):
        pl.semaphore_signal(barrier, inc=1, device_id=(device,), device_id_type=MESH)

    for step in (2, 4, 6, 250, 252, 254):
        greet(lax.rem(me + step, 256))

    def greet_group(i, carry):
        greet(lax.rem(p + i, 16) * 16 + q)
        greet(p * 16 + lax.rem(q + i, 16))
        return carry

    lax.fori_loop(1, 16, greet_group, 0)

    sent = []

    def copy(src, dst, ssem, rsem, device):
        return pltpu.make_async_remote_copy(
            src_ref=src, dst_ref=dst, send_sem=ssem, recv_sem=rsem,
            device_id=(device,), device_id_type=MESH,
        )

    def send(src, dst, ssem, rsem, device):
        c = copy(src, dst, ssem, rsem, device)
        c.start()
        sent.append(c)
        return c

    image_f = img_ref[...].astype(jnp.float32)
    image_inv = lax.rsqrt(jnp.sum(image_f * image_f, axis=-1, keepdims=True) + 1e-06)
    own_z = (image_f * image_inv).astype(jnp.bfloat16)
    imgs[0, 0] = own_z
    img_pair[0:B] = own_z
    ids[0] = jnp.concatenate(
        [
            jnp.broadcast_to(imgid_ref[...], (8, B)),
            jnp.broadcast_to(txtid_ref[...], (8, B)),
        ],
        axis=0,
    )
    feats[y, x] = txt_ref[...]

    pl.semaphore_wait(barrier, 36)

    H = B // 2

    def band_send(kind, buf, step, way, half):
        rows = pl.ds(half * H, H)
        src = buf.at[0, 0, rows] if step == 1 else buf.at[step - 1, way, rows]
        k = ((kind * 2 + way) * 3 + step - 1) * 2 + half
        return send(
            src, buf.at[step, way, rows], band_s.at[k], band_r.at[k], (right, left)[way]
        )

    hold = {}

    def band_start(kind, buf):
        for half in range(2):
            for way in range(2):
                hold[kind, 1, way, half] = band_send(kind, buf, 1, way, half)

    def band_forward(kind, buf, step):
        for half in range(2):
            for way in range(2):
                hold[kind, step, way, half].wait_recv()
                if step < 3:
                    hold[kind, step + 1, way, half] = band_send(kind, buf, step + 1, way, half)

    band_start(0, imgs)
    id_copies = []
    for n, step in enumerate((2, 4, 6)):
        for way in range(2):
            k = 2 * n + way
            to = lax.rem(me + (step if way == 0 else 256 - step), 256)
            id_copies.append(send(ids.at[0], ids.at[1 + k], id_s.at[k], id_r.at[k], to))
    id_copies.append(send(ids.at[0], ids.at[7], id_s.at[6], id_r.at[6], mate))
    img_mate = send(imgs.at[0, 0], img_pair.at[pl.ds(B, B)], pair_s.at[0], pair_r.at[0], mate)

    HX = XR // 2
    YR = B - XR
    HY = YR // 2
    own = feats.at[y, x]
    rx, ry = pl.ds(0, XR), pl.ds(XR, YR)
    f_sem = [0]

    def feat_send(src, device):
        k = f_sem[0]
        f_sem[0] += 1
        return send(src, src, fa_s.at[k], fa_r.at[k], device)

    fa1 = [
        feat_send(feats.at[y, x, rx], at(y, xp)),
        feat_send(feats.at[y, x, rx], at(y, xm)),
        feat_send(feats.at[y, x, ry], at(yp, x)),
        feat_send(feats.at[y, x, ry], at(ym, x)),
    ]

    def feats_second():
        for c in fa1:
            c.wait_recv()
        return [
            feat_send(feats.at[y, xm, pl.ds(0, HX)], at(y, xp)),
            feat_send(feats.at[y, xp, pl.ds(HX, HX)], at(y, xm)),
            feat_send(feats.at[ym, x, pl.ds(XR, HY)], at(yp, x)),
            feat_send(feats.at[yp, x, pl.ds(XR + HY, HY)], at(ym, x)),
        ]

    def feats_third(prev):
        for c in prev:
            c.wait_recv()
        return [
            feat_send(feats.at[y, :, rx], at(yp, x)),
            feat_send(feats.at[y, :, rx], at(ym, x)),
            feat_send(feats.at[:, x, ry], at(y, xp)),
            feat_send(feats.at[:, x, ry], at(y, xm)),
        ]

    def feats_fourth(prev):
        for c in prev:
            c.wait_recv()
        return [
            feat_send(feats.at[ym, :, pl.ds(0, HX)], at(yp, x)),
            feat_send(feats.at[yp, :, pl.ds(HX, HX)], at(ym, x)),
            feat_send(feats.at[:, xm, pl.ds(XR, HY)], at(y, xp)),
            feat_send(feats.at[:, xp, pl.ds(XR + HY, HY)], at(y, xm)),
        ]

    pre[...] = jnp.dot(txt_ref[...], head_ref[...], preferred_element_type=jnp.float32)
    text_pre = pre[...]
    text_inv = lax.rsqrt(jnp.sum(text_pre * text_pre, axis=-1, keepdims=True) + 1e-06)
    text_z = (text_pre * text_inv).astype(jnp.bfloat16)
    txts[0, 0] = text_z
    txt_pair[0:B] = text_z
    txt_mate = send(txts.at[0, 0], txt_pair.at[pl.ds(B, B)], pair_s.at[1], pair_r.at[1], mate)

    for c in id_copies:
        c.wait_recv()

    def column(row):
        return jnp.transpose(jnp.broadcast_to(row.astype(jnp.float32), (B, B)))

    for h, slot in ((0, 0), (1, 7)):
        img_col[pl.ds(h * B, B)] = column(ids[slot, 0:1])
        txt_col[pl.ds(h * B, B)] = column(ids[slot, 8:9])

    def process(kind, step, here_ref, col_ref, blocks, acc_ref):
        slots = (0,) if step == 0 else (2 * step - 1, 2 * step)
        logit = (
            10.0 * lax.dot_general(here_ref[...], blocks, NT, preferred_element_type=jnp.float32)
            - 5.0
        )
        coefs = []
        for n, slot in enumerate(slots):
            row = ids[slot, 8 * kind : 8 * kind + 1].astype(jnp.float32)
            label = jnp.where(col_ref[...] == row, 1.0, -1.0)
            part_logit = logit[:, n * B : (n + 1) * B]
            coef = -label * jax.nn.sigmoid(-label * part_logit)
            if step == 3:
                delta = 2 * step * (2 * n - 1)
                offset = (delta, delta + 2 * core - 1) if kind == 0 else (-delta, 1 - 2 * core - delta)
                keep = [
                    jnp.where((o >= 1 - REACH) & (o <= REACH), 1.0, 0.0).astype(jnp.float32)
                    for o in offset
                ]
                half = lax.broadcasted_iota(jnp.int32, coef.shape, 0) < B
                coef = coef * jnp.where(half, keep[0], keep[1])
            coefs.append(coef.astype(jnp.bfloat16))
        coef = coefs[0] if len(coefs) == 1 else jnp.concatenate(coefs, axis=1)
        term = jnp.dot(coef, blocks, preferred_element_type=jnp.float32)
        if step == 0:
            acc_ref[...] = term
        else:
            acc_ref[...] += term

    def pair_block(buf, step):
        return buf[step].reshape(2 * B, D)

    txt_mate.wait_recv()
    process(0, 0, txt_pair, txt_col, imgs[0, 0], acc_t)
    band_forward(0, imgs, 1)
    fa2 = feats_second()
    process(0, 1, txt_pair, txt_col, pair_block(imgs, 1), acc_t)
    band_forward(0, imgs, 2)
    band_start(1, txts)
    fa3 = feats_third(fa2)
    process(0, 2, txt_pair, txt_col, pair_block(imgs, 2), acc_t)
    img_mate.wait_recv()
    process(1, 0, img_pair, img_col, txts[0, 0], acc_i)
    band_forward(0, imgs, 3)
    process(0, 3, txt_pair, txt_col, pair_block(imgs, 3), acc_t)
    swap = send(acc_t.at[pl.ds(B, B)], got_t, pair_s.at[2], pair_r.at[2], mate)
    swap.wait_recv()
    grad_tz = 10.0 * (acc_t[0:B] + got_t[...])
    text_unit = pre[...] * text_inv
    grad_pre = (
        grad_tz - text_unit * jnp.sum(text_unit * grad_tz, axis=-1, keepdims=True)
    ) * text_inv
    for n in range(9):
        gp_t[n * B : (n + 1) * B] = jnp.transpose(grad_pre[:, n * B : (n + 1) * B]).astype(
            jnp.bfloat16
        )
    grad_pre = grad_pre.astype(jnp.bfloat16)

    def gp_copy(i):
        p2 = lax.rem(p + i, 16)
        return copy(
            gp_t.at[pl.ds(start_row(p2), SLICE)],
            gp_in.at[:, pl.ds(pl.multiple_of(p * B, B), B)],
            gp_s.at[i], gp_r.at[i], p2 * 16 + q,
        )

    def gp_send(i, carry):
        gp_copy(i).start()
        return carry

    lax.fori_loop(1, 16, gp_send, 0)
    gp_in[:, pl.ds(pl.multiple_of(p * B, B), B)] = gp_t[pl.ds(start_row(p), SLICE)]

    band_forward(1, txts, 1)
    fa4 = feats_fourth(fa3)
    process(1, 1, img_pair, img_col, pair_block(txts, 1), acc_i)
    gtxt_ref[...] = lax.dot_general(
        grad_pre, head_ref[...], NT, preferred_element_type=jnp.float32
    ).astype(jnp.bfloat16)
    band_forward(1, txts, 2)

    for c in fa4:
        c.wait_recv()

    def gp_wait(i, carry):
        gp_copy(i).wait_recv()
        return carry

    lax.fori_loop(1, 16, gp_wait, 0)
    slices = jnp.dot(gp_in[...], feats[...].reshape(16 * B, D), preferred_element_type=jnp.float32)
    for n in range(9):
        part[n] = slices[:, n * B : (n + 1) * B]

    def rs_copy(n, to):
        return copy(part.at[n], sums.at[q], rs_s.at[n], rs_r.at[q], p * 16 + to)

    for n, to in enumerate(OWNER):
        @pl.when(q != to)
        def _():
            rs_copy(n, to).start()

        @pl.when(q == to)
        def _():
            sums[q] = part[n]

    process(1, 2, img_pair, img_col, pair_block(txts, 2), acc_i)

    mine = jnp.where(core == 0, jnp.where(q == 2, 4, z // 2), 5 + z // 2)
    is_owner = jnp.logical_or(lax.rem(z, 2) == core, q == 2)
    lanes = pl.ds(pl.multiple_of(mine * B, B), B)

    def az_copy(i):
        z2 = lax.rem(z + i, 8)
        return copy(
            block, g_ref.at[y, x, :, lanes], az_s.at[i], az_r.at[mine], p * 16 + 2 * z2 + core
        )

    @pl.when(is_owner)
    def _():
        def rs_wait(i, carry):
            q2 = lax.rem(q + i, 16)
            copy(part.at[0], sums.at[q2], rs_s.at[0], rs_r.at[q2], mate).wait_recv()
            return carry

        lax.fori_loop(1, 16, rs_wait, 0)
        total = sums[0]
        for n in range(1, 16):
            total = total + sums[n]
        block[...] = total.astype(jnp.bfloat16)
        g_ref[y, x, :, lanes] = total.astype(jnp.bfloat16)

        def az_send(i, carry):
            az_copy(i).start()
            return carry

        lax.fori_loop(1, 8, az_send, 0)

    band_forward(1, txts, 3)
    process(1, 3, img_pair, img_col, pair_block(txts, 3), acc_i)
    swap_i = send(acc_i.at[pl.ds(B, B)], got_i, pair_s.at[3], pair_r.at[3], mate)

    def finish_image():
        swap_i.wait_recv()
        grad_iz = 10.0 * (acc_i[0:B] + got_i[...])
        image_g = img_ref[...].astype(jnp.float32)
        image_unit = image_g * image_inv
        gimg_ref[...] = (
            (grad_iz - image_unit * jnp.sum(image_unit * grad_iz, axis=-1, keepdims=True))
            * image_inv
        ).astype(jnp.bfloat16)

    def gather(cc):
        first, count = ((0, 5), (5, 4))[cc]
        for n in range(first, first + count):
            @pl.when(q != OWNER[n])
            def _():
                copy(
                    block, g_ref.at[y, x, :, pl.ds(n * B, B)], az_s.at[0], az_r.at[n], mate
                ).wait_recv()
        lx, ly = pl.ds(*X_LANES[cc]), pl.ds(*Y_LANES[cc])

        def mate_copy(k, view):
            return copy(view, view, am_s.at[k], am_r.at[k], mate)

        second = []
        for i in (1, 3, 2):
            x2, y2 = lax.rem(x + i, 4), lax.rem(y + i, 4)
            vx, vy = g_ref.at[y, x, :, lx], g_ref.at[y, x, :, ly]
            second.append(copy(vx, vx, a2_s.at[i], a2_r.at[i], at(y, x2)))
            second.append(copy(vy, vy, a2_s.at[4 + i], a2_r.at[4 + i], at(y2, x)))
        for c in second:
            c.start()
        finish_image()
        for c in second:
            c.wait_recv()
        third = []
        for i in (1, 3, 2):
            x2, y2 = lax.rem(x + i, 4), lax.rem(y + i, 4)
            vx, vy = g_ref.at[y, :, :, lx], g_ref.at[:, x, :, ly]
            third.append((i, copy(vx, vx, a3_s.at[i], a3_r.at[i], at(y2, x)),
                          copy(vy, vy, a3_s.at[4 + i], a3_r.at[4 + i], at(y, x2))))
        for i, a, b in third:
            a.start()
            b.start()
        mates = [mate_copy(0, g_ref.at[y, :, :, lx]), mate_copy(4, g_ref.at[:, x, :, ly])]
        for c in mates:
            c.start()
        for i, a, b in third:
            a.wait_recv()
            c = mate_copy(i, g_ref.at[lax.rem(y + 4 - i, 4), :, :, lx])
            c.start()
            mates.append(c)
            b.wait_recv()
            c = mate_copy(4 + i, g_ref.at[:, lax.rem(x + 4 - i, 4), :, ly])
            c.start()
            mates.append(c)
        for c in second:
            c.wait_send()
        for i, a, b in third:
            a.wait_send()
            b.wait_send()
        for c in mates:
            c.wait_send()
        other = 1 - cc
        ox, oy = pl.ds(*X_LANES[other]), pl.ds(*Y_LANES[other])
        for i in range(4):
            mate_copy(i, g_ref.at[lax.rem(y + 4 - i, 4), :, :, ox]).wait_recv()
            mate_copy(4 + i, g_ref.at[:, lax.rem(x + 4 - i, 4), :, oy]).wait_recv()

    for cc in range(2):
        @pl.when(core == cc)
        def _():
            gather(cc)

    for c in sent:
        c.wait_send()

    def gp_drain(i, carry):
        gp_copy(i).wait_send()
        return carry

    lax.fori_loop(1, 16, gp_drain, 0)
    for n, to in enumerate(OWNER):
        @pl.when(q != to)
        def _():
            rs_copy(n, to).wait_send()

    @pl.when(is_owner)
    def _():
        def az_drain(i, carry):
            az_copy(i).wait_send()
            return carry

        lax.fori_loop(1, 8, az_drain, 0)


def finish(g_ref, gimg_ref, gtxt_ref, oimg_ref, otxt_ref, ohead_ref, whole):
    @pl.when(pl.program_id(0) == 0)
    def _():
        oimg_ref[...] = gimg_ref[...]
        otxt_ref[...] = gtxt_ref[...]
        for p in range(16):
            if p % 2 == 0:
                whole[72 * p : 72 * p + 80] = g_ref[p // 4, p % 4]
            else:
                whole[72 * p + 8 : 72 * p + 72] = g_ref[p // 4, p % 4, 16:80]

    n = pl.program_id(0)
    eye = (
        lax.broadcasted_iota(jnp.int32, (B, B), 0) == lax.broadcasted_iota(jnp.int32, (B, B), 1)
    ).astype(jnp.bfloat16)
    ohead_ref[...] = lax.dot_general(
        eye, whole[:, pl.ds(pl.multiple_of(n * B, B), B)], NT, preferred_element_type=jnp.float32
    )


def shards(image_emb, image_ids, text_feats, text_ids, text_head):
    bf, f32 = jnp.bfloat16, jnp.float32
    vmem = pl.BlockSpec(memory_space=pltpu.VMEM)
    dma = pltpu.SemaphoreType.DMA
    scratch = [
        pltpu.VMEM((4, 2, B, D), bf),
        pltpu.VMEM((4, 2, B, D), bf),
        pltpu.VMEM((2 * B, D), bf),
        pltpu.VMEM((2 * B, D), bf),
        pltpu.VMEM((8, 16, B), jnp.int32),
        pltpu.VMEM((2 * B, B), f32),
        pltpu.VMEM((2 * B, B), f32),
        pltpu.VMEM((2 * B, D), f32),
        pltpu.VMEM((2 * B, D), f32),
        pltpu.VMEM((B, D), f32),
        pltpu.VMEM((B, D), f32),
        pltpu.VMEM((B, D), f32),
        pltpu.VMEM((D, B), bf),
        pltpu.VMEM((4, 4, B, D), bf),
        pltpu.VMEM((SLICE, 16 * B), bf),
        pltpu.VMEM((9, SLICE, B), f32),
        pltpu.VMEM((16, SLICE, B), f32),
        pltpu.VMEM((SLICE, B), bf),
    ]
    for n in (24, 7, 4, 16, 16):
        scratch += [dma((n,)), dma((n,))]
    scratch += [dma((9,)), dma((16,)), dma((8,)), dma((9,))]
    for n in (8, 8, 8):
        scratch += [dma((n,)), dma((n,))]
    gimg, gtxt, g = pl.pallas_call(
        kernel,
        out_shape=(
            jax.ShapeDtypeStruct((B, D), bf),
            jax.ShapeDtypeStruct((B, D), bf),
            jax.ShapeDtypeStruct((4, 4, SLICE, D), bf),
        ),
        in_specs=[vmem] * 5,
        out_specs=(vmem, vmem, vmem),
        scratch_shapes=scratch,
        compiler_params=pltpu.CompilerParams(
            collective_id=0, has_side_effects=True, vmem_limit_bytes=48 * 2**20
        ),
    )(image_emb, image_ids.reshape(1, B), text_feats, text_ids.reshape(1, B), text_head)
    fixed = pl.BlockSpec((B, D), lambda n: (0, 0))
    return pl.pallas_call(
        finish,
        grid=(9,),
        out_shape=(
            jax.ShapeDtypeStruct((B, D), bf),
            jax.ShapeDtypeStruct((B, D), bf),
            jax.ShapeDtypeStruct((D, D), f32),
        ),
        in_specs=[pl.BlockSpec((4, 4, SLICE, D), lambda n: (0, 0, 0, 0)), fixed, fixed],
        out_specs=(fixed, fixed, pl.BlockSpec((B, D), lambda n: (n, 0))),
        scratch_shapes=[pltpu.VMEM((D, D), bf)],
        compiler_params=pltpu.CompilerParams(vmem_limit_bytes=32 * 2**20),
    )(g, gimg, gtxt)


def solution(mesh):
    placed = (P("blk", None), P("blk"), P("blk", None), P("blk"), P())
    return jax.shard_map(
        shards,
        mesh=mesh,
        in_specs=placed,
        out_specs=(P("blk", None), P("blk", None), P()),
        check_vma=False,
    )
```

time: 614 us -> 140 us (0.23)
  waiting for transfers between devices: 476 us -> 0 us
  Pallas kernels: 0 us -> 132 us
  matrix products: 70.2 us -> 0 us
  starting transfers between devices: 22.7 us -> 0 us
  local copies, waits for them, and re-layouts: 25.4 us -> 6.8 us
  between operations: 14.2 us -> 0.66 us
    psum x1 -> x0, waiting for transfers between devices: 289 us -> none  [shards(): grad_head = lax.psum(head_term, 'blk')]
    ppermute x36 -> x0, waiting for transfers between devices: 187 us -> none  [from_behind(): return lax.ppermute(value, axis, pairs)]
    pallas_call x0 -> x2, Pallas kernels: none -> 132 us  [the longest x1 127 us: shards(): pl.pallas_call(kernel, out_shape=(jax.ShapeDtypeStruct((B, D), bf), jax.S...]
    dot_general x39 -> x0, matrix products: 70.2 us -> none  [the longest x12 24.8 us: pair_tile(): jnp.dot(coef, text_blk, preferred_element_type=jnp.float32)]
    ppermute x36 -> x0, starting transfers between devices: 22.6 us -> none  [from_behind(): return lax.ppermute(value, axis, pairs)]
    while x44 -> x0, local copies, waits for them, and re-layouts: 17 us -> none
  transfers between devices with their start and end apart: 37 -> 0, of which waited for: 14 -> 0; matrix products, arithmetic and copies ran while one was open for 5% -> 0% of each run, Pallas kernels for 0% -> 0%
where the time goes in v1:
time: 140 us
  Pallas kernels  132 us (94%)
  local copies, waits for them, and re-layouts  6.8 us (5%)
    pallas_call x1, Pallas kernels, shards(): pl.pallas_call(kernel, out_shape=(jax.ShapeDtypeStruct((B, D), bf), jax.S...  127 us
    unnamed x12, local copies, waits for them, and re-layouts  6.8 us
    pallas_call x1, Pallas kernels, shards(): pl.pallas_call(finish, grid=(9,), out_shape=(jax.ShapeDtypeStruct((B, D),...  5.5 us

profile of v1, /device:TPU:1, one launch (start us, length us, event | category | flops | bytes accessed | tf_op | source)
XLA Modules:
  0.0 139.9 jit_solution(11939490694367082483)
XLA Ops:
  0.6 0.0 copy-start.1
  0.6 1.7 %copy-done.1 = bf16[1152,1152]{1,0:T(8,128)(2,1)S(1)} copy-done((bf16[1152,1152]{1,0:T(8,128)(2,1)S(1)}, bf16[1152,1152]{1,0:T(8,128)(2,1)}, u32[]{:S(2)}) %copy-start.1) | copy-done | bytes 2654232
  2.4 0.0 copy-start.2
  2.4 1.0 copy-done.2
  3.3 0.0 copy-start.3
  3.3 1.0 copy-done.3
  4.3 0.0 copy-start.4
  4.3 0.7 copy-done.4
  5.0 0.0 copy-start.5
  5.0 0.7 copy-done.5
  5.6 127.0 %shard_map.76 = (bf16[128,1152]{1,0:T(8,128)(2,1)S(1)}, bf16[128,1152]{1,0:T(8,128)(2,1)S(1)}, bf16[4,4,80,1152]{3,2,1,0:T(8,128)(2,1)}) custom-call(bf16[128,1152]{1,0:T(8,128)(2,1)S(1)} %copy-done.2, s32[1,128]{1,0:T(1,128)S(1)} %bitcast.2, bf16[128,1152]{1,0:T(8,128)(2,1)S(1)} %copy-done.3, s32[1,128]{1,0:T(1,128)S(1)} %bitcast.3, ...), custom_call_target="tpu_custom_call" | custom-call | tf_op jit(solution)/shard_map/pallas_call | solution.py:479
  132.6 0.0 copy-start
  132.6 1.8 %copy-done = bf16[4,4,80,1152]{3,2,1,0:T(8,128)(2,1)S(1)} copy-done((bf16[4,4,80,1152]{3,2,1,0:T(8,128)(2,1)S(1)}, bf16[4,4,80,1152]{3,2,1,0:T(8,128)(2,1)}, u32[]{:S(2)}) %copy-start) | copy-done | bytes 2949144
  134.4 5.5 %shard_map.77 = (bf16[128,1152]{1,0:T(8,128)(2,1)}, bf16[128,1152]{1,0:T(8,128)(2,1)}, f32[1152,1152]{1,0:T(8,128)}) custom-call(bf16[4,4,80,1152]{3,2,1,0:T(8,128)(2,1)S(1)} %copy-done, bf16[128,1152]{1,0:T(8,128)(2,1)S(1)} %get-tuple-element.7.gimg_ref, bf16[128,1152]{1,0:T(8,128)(2,1)S(1)} %get-tuple-element.8.gtxt_ref), custom_call_target="tpu_custom_call" | custom-call | tf_op jit(solution)/shard_map/pallas_call | solution.py:494
Async XLA Ops:
  0.6 1.8 %copy-start.1 = (bf16[1152,1152]{1,0:T(8,128)(2,1)S(1)}, bf16[1152,1152]{1,0:T(8,128)(2,1)}, u32[]{:S(2)}) copy-start(bf16[1152,1152]{1,0:T(8,128)(2,1)} %head_ref.1) | copy-start | bytes 7962628
  2.4 1.0 copy-start.2
  3.3 1.0 copy-start.3
  4.3 0.7 copy-start.4
  5.0 0.7 copy-start.5
  132.6 1.8 %copy-start = (bf16[4,4,80,1152]{3,2,1,0:T(8,128)(2,1)S(1)}, bf16[4,4,80,1152]{3,2,1,0:T(8,128)(2,1)}, u32[]{:S(2)}) copy-start(bf16[4,4,80,1152]{3,2,1,0:T(8,128)(2,1)} %get-tuple-element.6.g_ref) | copy-start | bytes 8847364

commit v2 on v1

v2 whole, which is shorter than its diff:
```python
import jax
import jax.numpy as jnp
from jax import lax
from jax.experimental import pallas as pl
from jax.experimental.pallas import tpu as pltpu
from jax.sharding import PartitionSpec as P

MESH = pl.DeviceIdType.MESH
D = 1152
B = 128
REACH = 6
SLICE = 80
OWNER = (0, 4, 8, 12, 2, 3, 7, 11, 15)
X_LANES = ((256, 384), (640, 256))
X_ALL = (256, 640)
WIDE = 384
NT = (((1,), (1,)), ((), ()))


def start_row(a):
    return pl.multiple_of(16 * ((9 * a) // 2), 16)


def kernel(
    img_hbm, imgid_ref, txt_hbm, txtid_ref, head_hbm,
    gimg_ref, gtxt_ref, g_ref,
    img_ref, txt_ref, head_ref, imgs, txts, img_pair, txt_pair, ids, img_col, txt_col,
    acc_t, acc_i, got_t, got_i, pre, gp_t, feats, gp_in, part, sums, block,
    load, band_s, band_r, id_s, id_r, pair_s, pair_r, f_s, f_r, gp_s, gp_r, rs_s, rs_r,
    az_s, az_r, a2_s, a2_r, a3_s, a3_r, am_s, am_r,
):
    loads = [
        pltpu.make_async_copy(a, b, load.at[n])
        for n, (a, b) in enumerate(
            ((img_hbm, img_ref), (txt_hbm, txt_ref), (head_hbm, head_ref))
        )
    ]
    for c in loads:
        c.start()

    me = lax.axis_index("blk")
    core = lax.rem(me, 2)
    z = lax.rem(me // 2, 8)
    x = lax.rem(me // 16, 4)
    y = me // 64
    g, xp = x // 2, lax.rem(x, 2)
    a = (y * 2 + xp) * 2 + core
    b = z * 2 + g

    def at(y2, x2, z2, c2):
        return ((y2 * 4 + x2) * 8 + z2) * 2 + c2

    def of_group(a2):
        return at(a2 // 4, 2 * g + lax.rem(a2 // 2, 2), z, lax.rem(a2, 2))

    def of_column(b2):
        return at(y, 2 * lax.rem(b2, 2) + xp, b2 // 2, core)

    mate = at(y, x, z, 1 - core)
    partner = at(y, x + 1 - 2 * xp, z, core)
    right, left = lax.rem(me + 2, 256), lax.rem(me + 254, 256)
    yp, ym, yo = lax.rem(y + 1, 4), lax.rem(y + 3, 4), lax.rem(y + 2, 4)
    up, down = at(yp, x, z, core), at(ym, x, z, core)

    barrier = pltpu.get_barrier_semaphore()

    def greet(device):
        pl.semaphore_signal(barrier, inc=1, device_id=(device,), device_id_type=MESH)

    for step in (2, 4, 6, 250, 252, 254):
        greet(lax.rem(me + step, 256))
    greet(at(y, 3 - x, z, core))

    def greet_groups(i, carry):
        greet(of_group(lax.rem(a + i, 16)))
        greet(of_column(lax.rem(b + i, 16)))
        return carry

    lax.fori_loop(1, 16, greet_groups, 0)

    sent = []

    def copy(src, dst, ssem, rsem, device):
        return pltpu.make_async_remote_copy(
            src_ref=src, dst_ref=dst, send_sem=ssem, recv_sem=rsem,
            device_id=(device,), device_id_type=MESH,
        )

    def send(src, dst, ssem, rsem, device):
        c = copy(src, dst, ssem, rsem, device)
        c.start()
        sent.append(c)
        return c

    loads[0].wait()
    image_f = img_ref[...].astype(jnp.float32)
    image_inv = lax.rsqrt(jnp.sum(image_f * image_f, axis=-1, keepdims=True) + 1e-06)
    own_z = (image_f * image_inv).astype(jnp.bfloat16)
    imgs[0, 0] = own_z
    img_pair[0:B] = own_z
    ids[0] = jnp.concatenate(
        [
            jnp.broadcast_to(imgid_ref[...], (8, B)),
            jnp.broadcast_to(txtid_ref[...], (8, B)),
        ],
        axis=0,
    )
    loads[1].wait()
    feats[y, xp, core] = txt_ref[...]
    loads[2].wait()
    pre[...] = jnp.dot(txt_ref[...], head_ref[...], preferred_element_type=jnp.float32)
    text_pre = pre[...]
    text_inv = lax.rsqrt(jnp.sum(text_pre * text_pre, axis=-1, keepdims=True) + 1e-06)
    text_z = (text_pre * text_inv).astype(jnp.bfloat16)
    txts[0, 0] = text_z
    txt_pair[0:B] = text_z

    pl.semaphore_wait(barrier, 37)

    H = B // 2
    hold = {}

    def band_send(kind, buf, step, way, half):
        rows = pl.ds(half * H, H)
        src = buf.at[0, 0, rows] if step == 1 else buf.at[step - 1, way, rows]
        k = ((kind * 2 + way) * 3 + step - 1) * 2 + half
        hold[kind, step, way, half] = send(
            src, buf.at[step, way, rows], band_s.at[k], band_r.at[k], (right, left)[way]
        )

    def band_start(kind, buf):
        for half in range(2):
            for way in range(2):
                band_send(kind, buf, 1, way, half)

    def band_forward(kind, buf, step):
        for half in range(2):
            for way in range(2):
                hold[kind, step, way, half].wait_recv()
                if step < 3:
                    band_send(kind, buf, step + 1, way, half)

    def band_wait(kind, step):
        for half in range(2):
            for way in range(2):
                hold[kind, step, way, half].wait_recv()

    def band_pass(kind, buf, step):
        for half in range(2):
            for way in range(2):
                band_send(kind, buf, step + 1, way, half)

    band_start(0, imgs)
    txt_mate = send(txts.at[0, 0], txt_pair.at[pl.ds(B, B)], pair_s.at[1], pair_r.at[1], mate)
    id_copies = [send(ids.at[0], ids.at[7], id_s.at[6], id_r.at[6], mate)]
    for n, step in enumerate((2, 4, 6)):
        for way in range(2):
            k = 2 * n + way
            to = lax.rem(me + (step if way == 0 else 256 - step), 256)
            id_copies.append(send(ids.at[0], ids.at[1 + k], id_s.at[k], id_r.at[k], to))

    F = {}

    def feat_send(name, k, y2, xp2, device, rows=pl.ds(0, B)):
        view = feats.at[y2, xp2, core, rows]
        F[name] = send(view, view, f_s.at[k], f_r.at[k], device)

    low, high = pl.ds(0, H), pl.ds(H, H)
    other = 1 - xp
    feat_send("x", 0, y, xp, partner)
    feat_send("u", 1, y, xp, up)
    feat_send("d", 2, y, xp, down)
    img_mate = send(imgs.at[0, 0], img_pair.at[pl.ds(B, B)], pair_s.at[0], pair_r.at[0], mate)
    feat_send("m0", 8 + 0, y, xp, mate)

    def feats_second():
        F["x"].wait_recv()
        feat_send("xu", 3, y, other, up)
        feat_send("xd", 4, y, other, down)
        F["u"].wait_recv()
        feat_send("uu", 5, ym, xp, up, low)
        F["d"].wait_recv()
        feat_send("dd", 6, yp, xp, down, high)
        feat_send("m1", 8 + 1, y, other, mate)
        feat_send("m2", 8 + 2, ym, xp, mate)
        feat_send("m3", 8 + 3, yp, xp, mate)

    def feats_third():
        F["xu"].wait_recv()
        feat_send("xuu", 7, ym, other, up, low)
        F["xd"].wait_recv()
        feat_send("xdd", 16, yp, other, down, high)
        feat_send("m4", 8 + 4, ym, other, mate)
        feat_send("m5", 8 + 5, yp, other, mate)
        F["uu"].wait_recv()
        F["dd"].wait_recv()
        feat_send("m6", 8 + 6, yo, xp, mate)

    def feats_fourth():
        F["xuu"].wait_recv()
        F["xdd"].wait_recv()
        feat_send("m7", 8 + 7, yo, other, mate)

    def feats_wait():
        for n in range(8):
            F["m%d" % n].wait_recv()

    for c in id_copies:
        c.wait_recv()

    def column(row):
        return jnp.transpose(jnp.broadcast_to(row.astype(jnp.float32), (B, B)))

    for h, slot in ((0, 0), (1, 7)):
        img_col[pl.ds(h * B, B)] = column(ids[slot, 0:1])
        txt_col[pl.ds(h * B, B)] = column(ids[slot, 8:9])

    def process(kind, step, here_ref, col_ref, blocks, acc_ref):
        slots = (0,) if step == 0 else (2 * step - 1, 2 * step)
        logit = (
            10.0 * lax.dot_general(here_ref[...], blocks, NT, preferred_element_type=jnp.float32)
            - 5.0
        )
        coefs = []
        for n, slot in enumerate(slots):
            row = ids[slot, 8 * kind : 8 * kind + 1].astype(jnp.float32)
            label = jnp.where(col_ref[...] == row, 1.0, -1.0)
            part_logit = logit[:, n * B : (n + 1) * B]
            coef = -label * jax.nn.sigmoid(-label * part_logit)
            if step == 3:
                delta = 2 * step * (2 * n - 1)
                offset = (delta, delta + 2 * core - 1) if kind == 0 else (-delta, 1 - 2 * core - delta)
                keep = [
                    jnp.where((o >= 1 - REACH) & (o <= REACH), 1.0, 0.0).astype(jnp.float32)
                    for o in offset
                ]
                half = lax.broadcasted_iota(jnp.int32, coef.shape, 0) < B
                coef = coef * jnp.where(half, keep[0], keep[1])
            coefs.append(coef.astype(jnp.bfloat16))
        coef = coefs[0] if len(coefs) == 1 else jnp.concatenate(coefs, axis=1)
        term = jnp.dot(coef, blocks, preferred_element_type=jnp.float32)
        if step == 0:
            acc_ref[...] = term
        else:
            acc_ref[...] += term

    def pair_block(buf, step):
        return buf[step].reshape(2 * B, D)

    def process_images(step):
        process(0, step, txt_pair, txt_col, pair_block(imgs, step), acc_t)

    def process_texts(step):
        process(1, step, img_pair, img_col, pair_block(txts, step), acc_i)

    txt_mate.wait_recv()
    process(0, 0, txt_pair, txt_col, imgs[0, 0], acc_t)
    img_mate.wait_recv()
    process(1, 0, img_pair, img_col, txts[0, 0], acc_i)
    band_forward(0, imgs, 1)
    feats_second()
    process_images(1)
    band_forward(0, imgs, 2)
    band_start(1, txts)
    feats_third()
    process_images(2)
    band_wait(0, 3)
    process_images(3)
    swap = send(acc_t.at[pl.ds(B, B)], got_t, pair_s.at[2], pair_r.at[2], mate)
    text_unit = pre[...] * text_inv
    swap.wait_recv()
    grad_tz = 10.0 * (acc_t[0:B] + got_t[...])
    grad_pre = (
        grad_tz - text_unit * jnp.sum(text_unit * grad_tz, axis=-1, keepdims=True)
    ) * text_inv
    for n in range(9):
        gp_t[n * B : (n + 1) * B] = jnp.transpose(grad_pre[:, n * B : (n + 1) * B]).astype(
            jnp.bfloat16
        )
    grad_pre = grad_pre.astype(jnp.bfloat16)

    def gp_copy(i):
        a2 = lax.rem(a + i, 16)
        return copy(
            gp_t.at[pl.ds(start_row(a2), SLICE)],
            gp_in.at[:, pl.ds(pl.multiple_of(a * B, B), B)],
            gp_s.at[i], gp_r.at[i], of_group(a2),
        )

    def gp_send(i, carry):
        gp_copy(i).start()
        return carry

    lax.fori_loop(1, 16, gp_send, 0)
    gp_in[:, pl.ds(pl.multiple_of(a * B, B), B)] = gp_t[pl.ds(start_row(a), SLICE)]
    feats_fourth()
    gtxt_ref[...] = lax.dot_general(
        grad_pre, head_ref[...], NT, preferred_element_type=jnp.float32
    ).astype(jnp.bfloat16)
    band_forward(1, txts, 1)
    process_texts(1)
    feats_wait()

    def gp_wait(i, carry):
        gp_copy(i).wait_recv()
        return carry

    lax.fori_loop(1, 16, gp_wait, 0)
    slices = jnp.dot(gp_in[...], feats[...].reshape(16 * B, D), preferred_element_type=jnp.float32)
    for n in range(9):
        part[n] = slices[:, n * B : (n + 1) * B]

    def rs_copy(n, to):
        return copy(part.at[n], sums.at[b], rs_s.at[n], rs_r.at[b], of_column(to))

    for n, to in enumerate(OWNER):
        @pl.when(b != to)
        def _():
            rs_copy(n, to).start()

        @pl.when(b == to)
        def _():
            sums[b] = part[n]

    band_wait(1, 2)
    process_texts(2)

    mine = jnp.where(g == 0, jnp.where(b == 2, 4, z // 2), 5 + z // 2)
    is_owner = jnp.logical_or(lax.rem(z, 2) == g, b == 2)
    lanes = pl.ds(pl.multiple_of(mine * B, B), B)

    def az_copy(i):
        return copy(
            block, g_ref.at[y, xp, core, :, lanes], az_s.at[i], az_r.at[mine],
            at(y, x, lax.rem(z + i, 8), core),
        )

    def own_block():
        return pltpu.make_async_copy(block, g_ref.at[y, xp, core, :, lanes], load.at[0])

    @pl.when(is_owner)
    def _():
        def rs_wait(i, carry):
            b2 = lax.rem(b + i, 16)
            copy(part.at[0], sums.at[b2], rs_s.at[0], rs_r.at[b2], mate).wait_recv()
            return carry

        lax.fori_loop(1, 16, rs_wait, 0)
        total = sums[0]
        for n in range(1, 16):
            total = total + sums[n]
        block[...] = total.astype(jnp.bfloat16)

        def az_send(i, carry):
            az_copy(i).start()
            return carry

        lax.fori_loop(1, 8, az_send, 0)
        own_block().start()
        own_block().wait()

    for gg, (first, count) in enumerate(((0, 5), (5, 4))):
        for n in range(first, first + count):
            @pl.when((g == gg) & (b != OWNER[n]))
            def _():
                copy(
                    block, g_ref.at[y, xp, core, :, pl.ds(n * B, B)], az_s.at[0], az_r.at[n], mate
                ).wait_recv()

    def lanes_y(g2):
        return pl.ds(pl.multiple_of(896 * g2, B), 256)

    def back(x2, i):
        return lax.rem(x2 + 4 - i, 4)

    def along_x(i):
        return at(y, lax.rem(x + i, 4), z, core)

    def along_y(i):
        return at(lax.rem(y + i, 4), x, z, core)

    def second_x(i, gg):
        view = g_ref.at[y, xp, core, :, pl.ds(*X_LANES[gg])]
        return copy(view, view, a2_s.at[i], a2_r.at[i], along_x(i))

    def second_y(i):
        view = g_ref.at[y, xp, core, :, lanes_y(g)]
        return copy(view, view, a2_s.at[4 + i], a2_r.at[4 + i], along_y(i))

    def third_x(i):
        view = g_ref.at[y, :, core, :, pl.ds(*X_ALL)]
        return copy(view, view, a3_s.at[i], a3_r.at[i], along_y(i))

    def third_y(i):
        view = g_ref.at[:, xp, core, :, lanes_y(g)]
        return copy(view, view, a3_s.at[4 + i], a3_r.at[4 + i], along_x(i))

    def mate_x(i, c2):
        view = g_ref.at[back(y, i), :, c2, :, pl.ds(*X_ALL)]
        return copy(view, view, am_s.at[i], am_r.at[i], mate)

    def mate_y(i, c2):
        x2 = back(x, i)
        view = g_ref.at[:, lax.rem(x2, 2), c2, :, lanes_y(x2 // 2)]
        return copy(view, view, am_s.at[4 + i], am_r.at[4 + i], mate)

    ORDER = (1, 3, 2)
    for i in ORDER:
        for gg in range(2):
            @pl.when(g == gg)
            def _():
                second_x(i, gg).start()
        second_y(i).start()
    band_pass(1, txts, 2)
    for i in ORDER:
        for gg in range(2):
            @pl.when(back(x, i) // 2 == gg)
            def _():
                second_x(i, gg).wait_recv()
    for i in ORDER:
        third_x(i).start()
    for i in ORDER:
        second_y(i).wait_recv()
    for i in ORDER:
        third_y(i).start()
    mate_x(0, core).start()
    mate_y(0, core).start()

    band_wait(1, 3)
    process_texts(3)
    swap_i = send(acc_i.at[pl.ds(B, B)], got_i, pair_s.at[3], pair_r.at[3], mate)
    swap_i.wait_recv()
    grad_iz = 10.0 * (acc_i[0:B] + got_i[...])
    image_g = img_ref[...].astype(jnp.float32)
    image_unit = image_g * image_inv
    gimg_ref[...] = (
        (grad_iz - image_unit * jnp.sum(image_unit * grad_iz, axis=-1, keepdims=True)) * image_inv
    ).astype(jnp.bfloat16)

    for i in ORDER:
        third_x(i).wait_recv()
        mate_x(i, core).start()
        third_y(i).wait_recv()
        mate_y(i, core).start()

    for c in sent:
        c.wait_send()

    def gp_drain(i, carry):
        gp_copy(i).wait_send()
        return carry

    lax.fori_loop(1, 16, gp_drain, 0)
    for n, to in enumerate(OWNER):
        @pl.when(b != to)
        def _():
            rs_copy(n, to).wait_send()

    @pl.when(is_owner)
    def _():
        def az_drain(i, carry):
            az_copy(i).wait_send()
            return carry

        lax.fori_loop(1, 8, az_drain, 0)

    for i in ORDER:
        for gg in range(2):
            @pl.when(g == gg)
            def _():
                second_x(i, gg).wait_send()
        second_y(i).wait_send()
        third_x(i).wait_send()
        third_y(i).wait_send()
    for i in range(4):
        mate_x(i, core).wait_send()
        mate_y(i, core).wait_send()
        mate_x(i, 1 - core).wait_recv()
        mate_y(i, 1 - core).wait_recv()


def finish(g_ref, gimg_ref, gtxt_ref, oimg_ref, otxt_ref, ohead_ref, whole):
    @pl.when(pl.program_id(0) == 0)
    def _():
        oimg_ref[...] = gimg_ref[...]
        otxt_ref[...] = gtxt_ref[...]

    for a in range(16):
        view = g_ref[a // 4, (a // 2) % 2, a % 2]
        if a % 2 == 0:
            whole[72 * a : 72 * a + 80] = view
        else:
            whole[72 * a + 8 : 72 * a + 72] = view[16:80]
    eye = (
        lax.broadcasted_iota(jnp.int32, (B, B), 0) == lax.broadcasted_iota(jnp.int32, (B, B), 1)
    ).astype(jnp.bfloat16)
    for n in range(WIDE // B):
        ohead_ref[n * B : (n + 1) * B] = lax.dot_general(
            eye, whole[:, n * B : (n + 1) * B], NT, preferred_element_type=jnp.float32
        )


def shards(image_emb, image_ids, text_feats, text_ids, text_head):
    bf, f32 = jnp.bfloat16, jnp.float32
    vmem = pl.BlockSpec(memory_space=pltpu.VMEM)
    hbm = pl.BlockSpec(memory_space=pl.ANY)
    dma = pltpu.SemaphoreType.DMA
    scratch = [
        pltpu.VMEM((B, D), bf),
        pltpu.VMEM((B, D), bf),
        pltpu.VMEM((D, D), bf),
        pltpu.VMEM((4, 2, B, D), bf),
        pltpu.VMEM((4, 2, B, D), bf),
        pltpu.VMEM((2 * B, D), bf),
        pltpu.VMEM((2 * B, D), bf),
        pltpu.VMEM((8, 16, B), jnp.int32),
        pltpu.VMEM((2 * B, B), f32),
        pltpu.VMEM((2 * B, B), f32),
        pltpu.VMEM((2 * B, D), f32),
        pltpu.VMEM((2 * B, D), f32),
        pltpu.VMEM((B, D), f32),
        pltpu.VMEM((B, D), f32),
        pltpu.VMEM((B, D), f32),
        pltpu.VMEM((D, B), bf),
        pltpu.VMEM((4, 2, 2, B, D), bf),
        pltpu.VMEM((SLICE, 16 * B), bf),
        pltpu.VMEM((9, SLICE, B), f32),
        pltpu.VMEM((16, SLICE, B), f32),
        pltpu.VMEM((SLICE, B), bf),
        dma((3,)),
    ]
    for n in (24, 7, 4, 17, 16):
        scratch += [dma((n,)), dma((n,))]
    scratch += [dma((9,)), dma((16,)), dma((8,)), dma((9,))]
    for n in (8, 8, 8):
        scratch += [dma((n,)), dma((n,))]
    gimg, gtxt, g = pl.pallas_call(
        kernel,
        out_shape=(
            jax.ShapeDtypeStruct((B, D), bf),
            jax.ShapeDtypeStruct((B, D), bf),
            jax.ShapeDtypeStruct((4, 2, 2, SLICE, D), bf),
        ),
        in_specs=[hbm, vmem, hbm, vmem, hbm],
        out_specs=(vmem, vmem, hbm),
        scratch_shapes=scratch,
        compiler_params=pltpu.CompilerParams(
            collective_id=0, has_side_effects=True, vmem_limit_bytes=60 * 2**20
        ),
    )(image_emb, image_ids.reshape(1, B), text_feats, text_ids.reshape(1, B), text_head)
    fixed = pl.BlockSpec((B, D), lambda n: (0, 0))
    return pl.pallas_call(
        finish,
        grid=(D // WIDE,),
        out_shape=(
            jax.ShapeDtypeStruct((B, D), bf),
            jax.ShapeDtypeStruct((B, D), bf),
            jax.ShapeDtypeStruct((D, D), f32),
        ),
        in_specs=[pl.BlockSpec((4, 2, 2, SLICE, WIDE), lambda n: (0, 0, 0, 0, n)), fixed, fixed],
        out_specs=(fixed, fixed, pl.BlockSpec((WIDE, D), lambda n: (n, 0))),
        scratch_shapes=[pltpu.VMEM((D, WIDE), bf)],
        compiler_params=pltpu.CompilerParams(vmem_limit_bytes=60 * 2**20),
    )(g, gimg, gtxt)


def solution(mesh):
    placed = (P("blk", None), P("blk"), P("blk", None), P("blk"), P())
    return jax.shard_map(
        shards,
        mesh=mesh,
        in_specs=placed,
        out_specs=(P("blk", None), P("blk", None), P()),
        check_vma=False,
    )
```

time: 140 us -> 118 us (0.84)
  Pallas kernels: 132 us -> 118 us
  local copies, waits for them, and re-layouts: 6.8 us -> 0 us
    pallas_call x1, Pallas kernels: 127 us -> 112 us  [shards(): pl.pallas_call(kernel, out_shape=(jax.ShapeDtypeStruct((B, D), bf), jax.S...]
    unnamed x12 -> x0, local copies, waits for them, and re-layouts: 6.8 us -> none
where the time goes in v2:
time: 118 us
  Pallas kernels  118 us (100%)
    pallas_call x1, Pallas kernels, shards(): pl.pallas_call(kernel, out_shape=(jax.ShapeDtypeStruct((B, D), bf), jax.S...  112 us
    pallas_call x1, Pallas kernels, shards(): pl.pallas_call(finish, grid=(D // WIDE,), out_shape=(jax.ShapeDtypeStruct...  5.51 us

profile of v2, /device:TPU:1, one launch (start us, length us, event | category | flops | bytes accessed | tf_op | source)
XLA Modules:
  0.0 118.2 jit_solution(16258853010187200722)
XLA Ops:
  0.6 112.0 %shard_map.76 = (bf16[128,1152]{1,0:T(8,128)(2,1)}, bf16[128,1152]{1,0:T(8,128)(2,1)}, bf16[4,2,2,80,1152]{4,3,2,1,0:T(8,128)(2,1)}) custom-call(bf16[128,1152]{1,0:T(8,128)(2,1)} %img_hbm.1, s32[1,128]{1,0:T(1,128)} %bitcast.2, bf16[128,1152]{1,0:T(8,128)(2,1)} %txt_hbm.1, s32[1,128]{1,0:T(1,128)} %bitcast.3, bf16[1152,1152]{1,0:T(8,128)(2,1)} %head_hbm.1), custom_call_target="tpu_custom_call" | custom-call | tf_op jit(solution)/shard_map/pallas_call | solution.py:537
  112.7 5.5 %shard_map.77 = (bf16[128,1152]{1,0:T(8,128)(2,1)}, bf16[128,1152]{1,0:T(8,128)(2,1)}, f32[1152,1152]{1,0:T(8,128)}) custom-call(bf16[4,2,2,80,1152]{4,3,2,1,0:T(8,128)(2,1)} %get-tuple-element.6.g_ref, bf16[128,1152]{1,0:T(8,128)(2,1)} %get-tuple-element.7.gimg_ref, bf16[128,1152]{1,0:T(8,128)(2,1)} %get-tuple-element.8.gtxt_ref), custom_call_target="tpu_custom_call" | custom-call | tf_op jit(solution)/shard_map/pallas_call | solution.py:552

commit v3 on v2

--- a/solution.py
+++ b/solution.py
@@ -27,7 +27,7 @@
     img_ref, txt_ref, head_ref, imgs, txts, img_pair, txt_pair, ids, img_col, txt_col,
     acc_t, acc_i, got_t, got_i, pre, gp_t, feats, gp_in, part, sums, block,
     load, band_s, band_r, id_s, id_r, pair_s, pair_r, f_s, f_r, gp_s, gp_r, rs_s, rs_r,
-    az_s, az_r, a2_s, a2_r, a3_s, a3_r, am_s, am_r,
+    az_s, az_r, a2_s, a2_r, a3_s, a3_r, am_s, am_r, g_vm, keep,
 ):
     loads = [
         pltpu.make_async_copy(a, b, load.at[n])
@@ -115,42 +115,71 @@
     txts[0, 0] = text_z
     txt_pair[0:B] = text_z
 
+    @pl.when(core == 0)
+    def _():
+        imgs[3, 0] = jnp.zeros((B, D), jnp.bfloat16)
+
+    @pl.when(core == 1)
+    def _():
+        txts[3, 1] = jnp.zeros((B, D), jnp.bfloat16)
+
     pl.semaphore_wait(barrier, 37)
 
-    H = B // 2
     hold = {}
-
-    def band_send(kind, buf, step, way, half):
-        rows = pl.ds(half * H, H)
+    PARTS = (4, 2)
+
+    def idle(kind, step, way):
+        return step == 3 and way == kind
+
+    def wanted(kind):
+        return core == 1 if kind == 0 else core == 0
+
+    def band_copy(kind, buf, step, way, n):
+        rows = pl.ds(n * (B // PARTS[kind]), B // PARTS[kind])
         src = buf.at[0, 0, rows] if step == 1 else buf.at[step - 1, way, rows]
-        k = ((kind * 2 + way) * 3 + step - 1) * 2 + half
-        hold[kind, step, way, half] = send(
-            src, buf.at[step, way, rows], band_s.at[k], band_r.at[k], (right, left)[way]
-        )
-
-    def band_start(kind, buf):
-        for half in range(2):
+        k = ((kind * 2 + way) * 3 + step - 1) * 4 + n
+        return copy(src, buf.at[step, way, rows], band_s.at[k], band_r.at[k], (right, left)[way])
+
+    def band_send(kind, buf, step, way, n):
+        if idle(kind, step, way):
+            @pl.when(wanted(kind))
+            def _():
+                band_copy(kind, buf, step, way, n).start()
+            return
+        c = band_copy(kind, buf, step, way, n)
+        c.start()
+        sent.append(c)
+        hold[kind, step, way, n] = c
+
+    def band_start(kind, buf, first, last):
+        for n in range(first, last):
             for way in range(2):
-                band_send(kind, buf, 1, way, half)
+                band_send(kind, buf, 1, way, n)
+
+    def band_pace(n):
+        for way in range(2):
+            c = hold[0, 1, way, n]
+            c.wait_send()
+            sent.remove(c)
+            band_send(0, imgs, 1, way, n + 2)
 
     def band_forward(kind, buf, step):
-        for half in range(2):
+        for n in range(PARTS[kind]):
             for way in range(2):
-                hold[kind, step, way, half].wait_recv()
-                if step < 3:
-                    band_send(kind, buf, step + 1, way, half)
-
-    def band_wait(kind, step):
-        for half in range(2):
+                hold[kind, step, way, n].wait_recv()
+                band_send(kind, buf, step + 1, way, n)
+
+    def band_wait(kind, buf, step):
+        for n in range(PARTS[kind]):
             for way in range(2):
-                hold[kind, step, way, half].wait_recv()
-
-    def band_pass(kind, buf, step):
-        for half in range(2):
-            for way in range(2):
-                band_send(kind, buf, step + 1, way, half)
-
-    band_start(0, imgs)
+                if idle(kind, step, way):
+                    @pl.when(wanted(kind))
+                    def _():
+                        band_copy(kind, buf, step, way, n).wait_recv()
+                else:
+                    hold[kind, step, way, n].wait_recv()
+
+    band_start(0, imgs, 0, 2)
     txt_mate = send(txts.at[0, 0], txt_pair.at[pl.ds(B, B)], pair_s.at[1], pair_r.at[1], mate)
     id_copies = [send(ids.at[0], ids.at[7], id_s.at[6], id_r.at[6], mate)]
     for n, step in enumerate((2, 4, 6)):
@@ -161,11 +190,10 @@
 
     F = {}
 
-    def feat_send(name, k, y2, xp2, device, rows=pl.ds(0, B)):
-        view = feats.at[y2, xp2, core, rows]
+    def feat_send(name, k, y2, xp2, device):
+        view = feats.at[y2, xp2, core]
         F[name] = send(view, view, f_s.at[k], f_r.at[k], device)
 
-    low, high = pl.ds(0, H), pl.ds(H, H)
     other = 1 - xp
     feat_send("x", 0, y, xp, partner)
     feat_send("u", 1, y, xp, up)
@@ -173,32 +201,31 @@
     img_mate = send(imgs.at[0, 0], img_pair.at[pl.ds(B, B)], pair_s.at[0], pair_r.at[0], mate)
     feat_send("m0", 8 + 0, y, xp, mate)
 
+    over = jnp.where(g == 0, yp, ym)
+    across = jnp.where(g == 0, down, up)
+
     def feats_second():
         F["x"].wait_recv()
         feat_send("xu", 3, y, other, up)
         feat_send("xd", 4, y, other, down)
         F["u"].wait_recv()
-        feat_send("uu", 5, ym, xp, up, low)
         F["d"].wait_recv()
-        feat_send("dd", 6, yp, xp, down, high)
+        feat_send("o", 5, over, xp, across)
         feat_send("m1", 8 + 1, y, other, mate)
         feat_send("m2", 8 + 2, ym, xp, mate)
         feat_send("m3", 8 + 3, yp, xp, mate)
 
     def feats_third():
         F["xu"].wait_recv()
-        feat_send("xuu", 7, ym, other, up, low)
         F["xd"].wait_recv()
-        feat_send("xdd", 16, yp, other, down, high)
+        feat_send("xo", 6, over, other, across)
         feat_send("m4", 8 + 4, ym, other, mate)
         feat_send("m5", 8 + 5, yp, other, mate)
-        F["uu"].wait_recv()
-        F["dd"].wait_recv()
+        F["o"].wait_recv()
         feat_send("m6", 8 + 6, yo, xp, mate)
 
     def feats_fourth():
-        F["xuu"].wait_recv()
-        F["xdd"].wait_recv()
+        F["xo"].wait_recv()
         feat_send("m7", 8 + 7, yo, other, mate)
 
     def feats_wait():
@@ -253,18 +280,20 @@
     def process_texts(step):
         process(1, step, img_pair, img_col, pair_block(txts, step), acc_i)
 
+    band_pace(0)
     txt_mate.wait_recv()
     process(0, 0, txt_pair, txt_col, imgs[0, 0], acc_t)
+    band_pace(1)
     img_mate.wait_recv()
     process(1, 0, img_pair, img_col, txts[0, 0], acc_i)
     band_forward(0, imgs, 1)
     feats_second()
     process_images(1)
     band_forward(0, imgs, 2)
-    band_start(1, txts)
     feats_third()
     process_images(2)
-    band_wait(0, 3)
+    band_wait(0, imgs, 3)
+    band_start(1, txts, 0, 2)
     process_images(3)
     swap = send(acc_t.at[pl.ds(B, B)], got_t, pair_s.at[2], pair_r.at[2], mate)
     text_unit = pre[...] * text_inv
@@ -322,21 +351,17 @@
         def _():
             sums[b] = part[n]
 
-    band_wait(1, 2)
+    band_forward(1, txts, 2)
     process_texts(2)
-
     mine = jnp.where(g == 0, jnp.where(b == 2, 4, z // 2), 5 + z // 2)
     is_owner = jnp.logical_or(lax.rem(z, 2) == g, b == 2)
     lanes = pl.ds(pl.multiple_of(mine * B, B), B)
 
     def az_copy(i):
         return copy(
-            block, g_ref.at[y, xp, core, :, lanes], az_s.at[i], az_r.at[mine],
+            block, g_vm.at[y, xp, core, :, lanes], az_s.at[i], az_r.at[mine],
             at(y, x, lax.rem(z + i, 8), core),
         )
-
-    def own_block():
-        return pltpu.make_async_copy(block, g_ref.at[y, xp, core, :, lanes], load.at[0])
 
     @pl.when(is_owner)
     def _():
@@ -350,21 +375,20 @@
         for n in range(1, 16):
             total = total + sums[n]
         block[...] = total.astype(jnp.bfloat16)
+        g_vm[y, xp, core, :, lanes] = total.astype(jnp.bfloat16)
 
         def az_send(i, carry):
             az_copy(i).start()
             return carry
 
         lax.fori_loop(1, 8, az_send, 0)
-        own_block().start()
-        own_block().wait()
 
     for gg, (first, count) in enumerate(((0, 5), (5, 4))):
         for n in range(first, first + count):
             @pl.when((g == gg) & (b != OWNER[n]))
             def _():
                 copy(
-                    block, g_ref.at[y, xp, core, :, pl.ds(n * B, B)], az_s.at[0], az_r.at[n], mate
+                    block, g_vm.at[y, xp, core, :, pl.ds(n * B, B)], az_s.at[0], az_r.at[n], mate
                 ).wait_recv()
 
     def lanes_y(g2):
@@ -380,29 +404,43 @@
         return at(lax.rem(y + i, 4), x, z, core)
 
     def second_x(i, gg):
-        view = g_ref.at[y, xp, core, :, pl.ds(*X_LANES[gg])]
+        view = g_vm.at[y, xp, core, :, pl.ds(*X_LANES[gg])]
         return copy(view, view, a2_s.at[i], a2_r.at[i], along_x(i))
 
     def second_y(i):
-        view = g_ref.at[y, xp, core, :, lanes_y(g)]
+        view = g_vm.at[y, xp, core, :, lanes_y(g)]
         return copy(view, view, a2_s.at[4 + i], a2_r.at[4 + i], along_y(i))
 
     def third_x(i):
-        view = g_ref.at[y, :, core, :, pl.ds(*X_ALL)]
+        view = g_vm.at[y, :, core, :, pl.ds(*X_ALL)]
         return copy(view, view, a3_s.at[i], a3_r.at[i], along_y(i))
 
     def third_y(i):
-        view = g_ref.at[:, xp, core, :, lanes_y(g)]
+        view = g_vm.at[:, xp, core, :, lanes_y(g)]
         return copy(view, view, a3_s.at[4 + i], a3_r.at[4 + i], along_x(i))
 
+    def place_x(ref, i, c2):
+        return ref.at[back(y, i), :, c2, :, pl.ds(*X_ALL)]
+
+    def place_y(ref, i, c2):
+        x2 = back(x, i)
+        return ref.at[:, lax.rem(x2, 2), c2, :, lanes_y(x2 // 2)]
+
     def mate_x(i, c2):
-        view = g_ref.at[back(y, i), :, c2, :, pl.ds(*X_ALL)]
-        return copy(view, view, am_s.at[i], am_r.at[i], mate)
+        return copy(place_x(g_vm, i, c2), place_x(g_ref, i, c2), am_s.at[i], am_r.at[i], mate)
 
     def mate_y(i, c2):
-        x2 = back(x, i)
-        view = g_ref.at[:, lax.rem(x2, 2), c2, :, lanes_y(x2 // 2)]
-        return copy(view, view, am_s.at[4 + i], am_r.at[4 + i], mate)
+        return copy(
+            place_y(g_vm, i, c2), place_y(g_ref, i, c2), am_s.at[4 + i], am_r.at[4 + i], mate
+        )
+
+    def keep_x(i):
+        return pltpu.make_async_copy(place_x(g_vm, i, core), place_x(g_ref, i, core), keep.at[i])
+
+    def keep_y(i):
+        return pltpu.make_async_copy(
+            place_y(g_vm, i, core), place_y(g_ref, i, core), keep.at[4 + i]
+        )
 
     ORDER = (1, 3, 2)
     for i in ORDER:
@@ -411,7 +449,6 @@
             def _():
                 second_x(i, gg).start()
         second_y(i).start()
-    band_pass(1, txts, 2)
     for i in ORDER:
         for gg in range(2):
             @pl.when(back(x, i) // 2 == gg)
@@ -424,11 +461,32 @@
     for i in ORDER:
         third_y(i).start()
     mate_x(0, core).start()
+    keep_x(0).start()
     mate_y(0, core).start()
-
-    band_wait(1, 3)
+    keep_y(0).start()
+
+
+    band_wait(1, txts, 3)
     process_texts(3)
     swap_i = send(acc_i.at[pl.ds(B, B)], got_i, pair_s.at[3], pair_r.at[3], mate)
+    third_x(1).wait_recv()
+    mate_x(1, core).start()
+    keep_x(1).start()
+    third_y(1).wait_recv()
+    mate_y(1, core).start()
+    keep_y(1).start()
+    third_x(3).wait_recv()
+    mate_x(3, core).start()
+    keep_x(3).start()
+    third_y(3).wait_recv()
+    mate_y(3, core).start()
+    keep_y(3).start()
+    third_x(2).wait_recv()
+    mate_x(2, core).start()
+    keep_x(2).start()
+    third_y(2).wait_recv()
+    mate_y(2, core).start()
+    keep_y(2).start()
     swap_i.wait_recv()
     grad_iz = 10.0 * (acc_i[0:B] + got_i[...])
     image_g = img_ref[...].astype(jnp.float32)
@@ -437,12 +495,11 @@
         (grad_iz - image_unit * jnp.sum(image_unit * grad_iz, axis=-1, keepdims=True)) * image_inv
     ).astype(jnp.bfloat16)
 
-    for i in ORDER:
-        third_x(i).wait_recv()
-        mate_x(i, core).start()
-        third_y(i).wait_recv()
-        mate_y(i, core).start()
-
+    for kind, buf in ((0, imgs), (1, txts)):
+        @pl.when(wanted(kind))
+        def _():
+            for n in range(PARTS[kind]):
+                band_copy(kind, buf, 3, kind, n).wait_send()
     for c in sent:
         c.wait_send()
 
@@ -473,6 +530,8 @@
         third_x(i).wait_send()
         third_y(i).wait_send()
     for i in range(4):
+        keep_x(i).wait()
+        keep_y(i).wait()
         mate_x(i, core).wait_send()
         mate_y(i, core).wait_send()
         mate_x(i, 1 - core).wait_recv()
@@ -491,12 +550,13 @@
             whole[72 * a : 72 * a + 80] = view
         else:
             whole[72 * a + 8 : 72 * a + 72] = view[16:80]
-    eye = (
-        lax.broadcasted_iota(jnp.int32, (B, B), 0) == lax.broadcasted_iota(jnp.int32, (B, B), 1)
-    ).astype(jnp.bfloat16)
-    for n in range(WIDE // B):
-        ohead_ref[n * B : (n + 1) * B] = lax.dot_general(
-            eye, whole[:, n * B : (n + 1) * B], NT, preferred_element_type=jnp.float32
+    for start, size in ((0, 256), (256, 128)):
+        eye = lax.broadcasted_iota(jnp.int32, (size, size), 0) == lax.broadcasted_iota(
+            jnp.int32, (size, size), 1
+        )
+        ohead_ref[start : start + size] = lax.dot_general(
+            eye.astype(jnp.bfloat16), whole[:, start : start + size], NT,
+            preferred_element_type=jnp.float32,
         )
 
 
@@ -529,11 +589,12 @@
         pltpu.VMEM((SLICE, B), bf),
         dma((3,)),
     ]
-    for n in (24, 7, 4, 17, 16):
+    for n in (48, 7, 4, 16, 16):
         scratch += [dma((n,)), dma((n,))]
     scratch += [dma((9,)), dma((16,)), dma((8,)), dma((9,))]
     for n in (8, 8, 8):
         scratch += [dma((n,)), dma((n,))]
+    scratch += [pltpu.VMEM((4, 2, 2, SLICE, D), bf), dma((8,))]
     gimg, gtxt, g = pl.pallas_call(
         kernel,
         out_shape=(

time: 118 us -> 107 us (0.907)
  Pallas kernels: 118 us -> 106 us
    pallas_call x1, Pallas kernels: 112 us -> 101 us  [shards(): pl.pallas_call(kernel, out_shape=(jax.ShapeDtypeStruct((B, D), bf), jax.S...]
where the time goes in v3:
time: 107 us
  Pallas kernels  106 us (99%)
    pallas_call x1, Pallas kernels, shards(): pl.pallas_call(kernel, out_shape=(jax.ShapeDtypeStruct((B, D), bf), jax.S...  101 us
    pallas_call x1, Pallas kernels, shards(): pl.pallas_call(finish, grid=(D // WIDE,), out_shape=(jax.ShapeDtypeStruct...  5.52 us

profile of v3, /device:TPU:1, one launch (start us, length us, event | category | flops | bytes accessed | tf_op | source)
XLA Modules:
  0.0 106.9 jit_solution(14111219374631009136)
XLA Ops:
  0.6 100.7 %shard_map.76 = (bf16[128,1152]{1,0:T(8,128)(2,1)}, bf16[128,1152]{1,0:T(8,128)(2,1)}, bf16[4,2,2,80,1152]{4,3,2,1,0:T(8,128)(2,1)}) custom-call(bf16[128,1152]{1,0:T(8,128)(2,1)} %img_hbm.1, s32[1,128]{1,0:T(1,128)} %bitcast.2, bf16[128,1152]{1,0:T(8,128)(2,1)} %txt_hbm.1, s32[1,128]{1,0:T(1,128)} %bitcast.3, bf16[1152,1152]{1,0:T(8,128)(2,1)} %head_hbm.1), custom_call_target="tpu_custom_call" | custom-call | tf_op jit(solution)/shard_map/pallas_call | solution.py:598
  101.3 5.5 %shard_map.77 = (bf16[128,1152]{1,0:T(8,128)(2,1)}, bf16[128,1152]{1,0:T(8,128)(2,1)}, f32[1152,1152]{1,0:T(8,128)}) custom-call(bf16[4,2,2,80,1152]{4,3,2,1,0:T(8,128)(2,1)} %get-tuple-element.6.g_ref, bf16[128,1152]{1,0:T(8,128)(2,1)} %get-tuple-element.7.gimg_ref, bf16[128,1152]{1,0:T(8,128)(2,1)} %get-tuple-element.8.gtxt_ref), custom_call_target="tpu_custom_call" | custom-call | tf_op jit(solution)/shard_map/pallas_call | solution.py:613

commit v4 on v3

--- a/solution.py
+++ b/solution.py
@@ -107,21 +107,6 @@
     )
     loads[1].wait()
     feats[y, xp, core] = txt_ref[...]
-    loads[2].wait()
-    pre[...] = jnp.dot(txt_ref[...], head_ref[...], preferred_element_type=jnp.float32)
-    text_pre = pre[...]
-    text_inv = lax.rsqrt(jnp.sum(text_pre * text_pre, axis=-1, keepdims=True) + 1e-06)
-    text_z = (text_pre * text_inv).astype(jnp.bfloat16)
-    txts[0, 0] = text_z
-    txt_pair[0:B] = text_z
-
-    @pl.when(core == 0)
-    def _():
-        imgs[3, 0] = jnp.zeros((B, D), jnp.bfloat16)
-
-    @pl.when(core == 1)
-    def _():
-        txts[3, 1] = jnp.zeros((B, D), jnp.bfloat16)
 
     pl.semaphore_wait(barrier, 37)
 
@@ -180,7 +165,6 @@
                     hold[kind, step, way, n].wait_recv()
 
     band_start(0, imgs, 0, 2)
-    txt_mate = send(txts.at[0, 0], txt_pair.at[pl.ds(B, B)], pair_s.at[1], pair_r.at[1], mate)
     id_copies = [send(ids.at[0], ids.at[7], id_s.at[6], id_r.at[6], mate)]
     for n, step in enumerate((2, 4, 6)):
         for way in range(2):
@@ -190,47 +174,103 @@
 
     F = {}
 
-    def feat_send(name, k, y2, xp2, device):
-        view = feats.at[y2, xp2, core]
-        F[name] = send(view, view, f_s.at[k], f_r.at[k], device)
-
+    def feat_copy(k, y2, xp2, device, rows=pl.ds(0, B), arrival=None):
+        view = feats.at[y2, xp2, core, rows]
+        return copy(view, view, f_s.at[k], f_r.at[k if arrival is None else arrival], device)
+
+    def feat_send(name, *place):
+        F[name] = feat_copy(*place)
+        F[name].start()
+        sent.append(F[name])
+
+    maybe = []
+
+    def feat_when(cond, name, *place):
+        c = F[name] = feat_copy(*place)
+
+        @pl.when(cond)
+        def _():
+            c.start()
+
+        maybe.append((cond, c))
+
+    up_shut, up_help = (x == 0) & (z == 0), (x == 1) & (z == 0)
+    down_shut, down_help = (x == 3) & (z == 7), (x == 2) & (z == 7)
+    up_open, down_open = jnp.logical_not(up_shut), jnp.logical_not(down_shut)
     other = 1 - xp
     feat_send("x", 0, y, xp, partner)
-    feat_send("u", 1, y, xp, up)
-    feat_send("d", 2, y, xp, down)
+    feat_when(up_open, "u", 1, y, xp, up)
+    feat_when(down_open, "d", 2, y, xp, down)
     img_mate = send(imgs.at[0, 0], img_pair.at[pl.ds(B, B)], pair_s.at[0], pair_r.at[0], mate)
     feat_send("m0", 8 + 0, y, xp, mate)
 
-    over = jnp.where(g == 0, yp, ym)
-    across = jnp.where(g == 0, down, up)
+    low, high = pl.ds(0, B // 2), pl.ds(B // 2, B // 2)
 
     def feats_second():
         F["x"].wait_recv()
-        feat_send("xu", 3, y, other, up)
-        feat_send("xd", 4, y, other, down)
+        feat_when(up_open, "xu", 3, y, other, up)
+        feat_when(down_open, "xd", 4, y, other, down)
+        feat_send("m1", 8 + 1, y, other, mate)
+
+    def feats_up():
         F["u"].wait_recv()
+        F["xu"].wait_recv()
+        F["m2"].start()
+        F["m4"].start()
+
+    def feats_down():
         F["d"].wait_recv()
-        feat_send("o", 5, over, xp, across)
-        feat_send("m1", 8 + 1, y, other, mate)
-        feat_send("m2", 8 + 2, ym, xp, mate)
-        feat_send("m3", 8 + 3, yp, xp, mate)
+        F["xd"].wait_recv()
+        F["m3"].start()
+        F["m5"].start()
 
     def feats_third():
-        F["xu"].wait_recv()
-        F["xd"].wait_recv()
-        feat_send("xo", 6, over, other, across)
-        feat_send("m4", 8 + 4, ym, other, mate)
-        feat_send("m5", 8 + 5, yp, other, mate)
-        F["o"].wait_recv()
+        for k, y2, xp2 in ((2, ym, xp), (3, yp, xp), (4, ym, other), (5, yp, other)):
+            F["m%d" % k] = feat_copy(8 + k, y2, xp2, mate)
+            sent.append(F["m%d" % k])
+        pl.when(up_open)(feats_up)
+        pl.when(down_open)(feats_down)
+        low_from, low_to = jnp.where(up_shut, yp, ym), jnp.where(up_shut, down, up)
+        high_from, high_to = jnp.where(down_shut, ym, yp), jnp.where(down_shut, up, down)
+        feat_send("o0", 5, low_from, xp, low_to, low)
+        feat_send("o1", 6, high_from, xp, high_to, high)
+        feat_send("xo0", 7, low_from, other, low_to, low)
+        feat_send("xo1", 16, high_from, other, high_to, high)
+        feat_when(up_help, "hu0", 17, ym, xp, partner, pl.ds(0, B), 3)
+        feat_when(up_help, "hu1", 18, ym, other, partner, pl.ds(0, B), 1)
+        feat_when(down_help, "hd0", 19, yp, xp, partner, pl.ds(0, B), 4)
+        feat_when(down_help, "hd1", 20, yp, other, partner, pl.ds(0, B), 2)
+
+    def feats_fourth():
+        F["o0"].wait_recv()
+        F["o1"].wait_recv()
         feat_send("m6", 8 + 6, yo, xp, mate)
-
-    def feats_fourth():
-        F["xo"].wait_recv()
+        F["xo0"].wait_recv()
+        F["xo1"].wait_recv()
         feat_send("m7", 8 + 7, yo, other, mate)
+        pl.when(up_shut)(feats_up)
+        pl.when(down_shut)(feats_down)
 
     def feats_wait():
         for n in range(8):
             F["m%d" % n].wait_recv()
+
+    @pl.when(core == 0)
+    def _():
+        imgs[3, 0] = jnp.zeros((B, D), jnp.bfloat16)
+
+    @pl.when(core == 1)
+    def _():
+        txts[3, 1] = jnp.zeros((B, D), jnp.bfloat16)
+
+    loads[2].wait()
+    pre[...] = jnp.dot(txt_ref[...], head_ref[...], preferred_element_type=jnp.float32)
+    text_pre = pre[...]
+    text_inv = lax.rsqrt(jnp.sum(text_pre * text_pre, axis=-1, keepdims=True) + 1e-06)
+    text_z = (text_pre * text_inv).astype(jnp.bfloat16)
+    txts[0, 0] = text_z
+    txt_pair[0:B] = text_z
+    txt_mate = send(txts.at[0, 0], txt_pair.at[pl.ds(B, B)], pair_s.at[1], pair_r.at[1], mate)
 
     for c in id_copies:
         c.wait_recv()
@@ -327,7 +367,6 @@
         grad_pre, head_ref[...], NT, preferred_element_type=jnp.float32
     ).astype(jnp.bfloat16)
     band_forward(1, txts, 1)
-    process_texts(1)
     feats_wait()
 
     def gp_wait(i, carry):
@@ -337,7 +376,7 @@
     lax.fori_loop(1, 16, gp_wait, 0)
     slices = jnp.dot(gp_in[...], feats[...].reshape(16 * B, D), preferred_element_type=jnp.float32)
     for n in range(9):
-        part[n] = slices[:, n * B : (n + 1) * B]
+        part[n] = slices[:, n * B : (n + 1) * B].astype(jnp.bfloat16)
 
     def rs_copy(n, to):
         return copy(part.at[n], sums.at[b], rs_s.at[n], rs_r.at[b], of_column(to))
@@ -351,8 +390,8 @@
         def _():
             sums[b] = part[n]
 
+    process_texts(1)
     band_forward(1, txts, 2)
-    process_texts(2)
     mine = jnp.where(g == 0, jnp.where(b == 2, 4, z // 2), 5 + z // 2)
     is_owner = jnp.logical_or(lax.rem(z, 2) == g, b == 2)
     lanes = pl.ds(pl.multiple_of(mine * B, B), B)
@@ -371,9 +410,9 @@
             return carry
 
         lax.fori_loop(1, 16, rs_wait, 0)
-        total = sums[0]
+        total = sums[0].astype(jnp.float32)
         for n in range(1, 16):
-            total = total + sums[n]
+            total = total + sums[n].astype(jnp.float32)
         block[...] = total.astype(jnp.bfloat16)
         g_vm[y, xp, core, :, lanes] = total.astype(jnp.bfloat16)
 
@@ -449,6 +488,7 @@
             def _():
                 second_x(i, gg).start()
         second_y(i).start()
+    process_texts(2)
     for i in ORDER:
         for gg in range(2):
             @pl.when(back(x, i) // 2 == gg)
@@ -495,6 +535,8 @@
         (grad_iz - image_unit * jnp.sum(image_unit * grad_iz, axis=-1, keepdims=True)) * image_inv
     ).astype(jnp.bfloat16)
 
+    for cond, c in maybe:
+        pl.when(cond)(c.wait_send)
     for kind, buf in ((0, imgs), (1, txts)):
         @pl.when(wanted(kind))
         def _():
@@ -584,12 +626,12 @@
         pltpu.VMEM((D, B), bf),
         pltpu.VMEM((4, 2, 2, B, D), bf),
         pltpu.VMEM((SLICE, 16 * B), bf),
-        pltpu.VMEM((9, SLICE, B), f32),
-        pltpu.VMEM((16, SLICE, B), f32),
+        pltpu.VMEM((9, SLICE, B), bf),
+        pltpu.VMEM((16, SLICE, B), bf),
         pltpu.VMEM((SLICE, B), bf),
         dma((3,)),
     ]
-    for n in (48, 7, 4, 16, 16):
+    for n in (48, 7, 4, 21, 16):
         scratch += [dma((n,)), dma((n,))]
     scratch += [dma((9,)), dma((16,)), dma((8,)), dma((9,))]
     for n in (8, 8, 8):

time: 107 us -> 102 us (0.953)
  Pallas kernels: 106 us -> 102 us
    pallas_call x1, Pallas kernels: 101 us -> 96.1 us  [shards(): pl.pallas_call(kernel, out_shape=(jax.ShapeDtypeStruct((B, D), bf), jax.S...]
where the time goes in v4:
time: 102 us
  Pallas kernels  102 us (100%)
    pallas_call x1, Pallas kernels, shards(): pl.pallas_call(kernel, out_shape=(jax.ShapeDtypeStruct((B, D), bf), jax.S...  96.1 us
    pallas_call x1, Pallas kernels, shards(): pl.pallas_call(finish, grid=(D // WIDE,), out_shape=(jax.ShapeDtypeStruct...  5.53 us

profile of v4, /device:TPU:1, one launch (start us, length us, event | category | flops | bytes accessed | tf_op | source)
XLA Modules:
  0.0 102.2 jit_solution(15396325657891800582)
XLA Ops:
  0.6 96.1 %shard_map.76 = (bf16[128,1152]{1,0:T(8,128)(2,1)}, bf16[128,1152]{1,0:T(8,128)(2,1)}, bf16[4,2,2,80,1152]{4,3,2,1,0:T(8,128)(2,1)}) custom-call(bf16[128,1152]{1,0:T(8,128)(2,1)} %img_hbm.1, s32[1,128]{1,0:T(1,128)} %bitcast.2, bf16[128,1152]{1,0:T(8,128)(2,1)} %txt_hbm.1, s32[1,128]{1,0:T(1,128)} %bitcast.3, bf16[1152,1152]{1,0:T(8,128)(2,1)} %head_hbm.1), custom_call_target="tpu_custom_call" | custom-call | tf_op jit(solution)/shard_map/pallas_call | solution.py:640
  96.7 5.5 %shard_map.77 = (bf16[128,1152]{1,0:T(8,128)(2,1)}, bf16[128,1152]{1,0:T(8,128)(2,1)}, f32[1152,1152]{1,0:T(8,128)}) custom-call(bf16[4,2,2,80,1152]{4,3,2,1,0:T(8,128)(2,1)} %get-tuple-element.6.g_ref, bf16[128,1152]{1,0:T(8,128)(2,1)} %get-tuple-element.7.gimg_ref, bf16[128,1152]{1,0:T(8,128)(2,1)} %get-tuple-element.8.gtxt_ref), custom_call_target="tpu_custom_call" | custom-call | tf_op jit(solution)/shard_map/pallas_call | solution.py:655

commit v5 on v4

--- a/solution.py
+++ b/solution.py
@@ -362,11 +362,11 @@
 
     lax.fori_loop(1, 16, gp_send, 0)
     gp_in[:, pl.ds(pl.multiple_of(a * B, B), B)] = gp_t[pl.ds(start_row(a), SLICE)]
+    band_forward(1, txts, 1)
     feats_fourth()
     gtxt_ref[...] = lax.dot_general(
         grad_pre, head_ref[...], NT, preferred_element_type=jnp.float32
     ).astype(jnp.bfloat16)
-    band_forward(1, txts, 1)
     feats_wait()
 
     def gp_wait(i, carry):
@@ -374,21 +374,23 @@
         return carry
 
     lax.fori_loop(1, 16, gp_wait, 0)
-    slices = jnp.dot(gp_in[...], feats[...].reshape(16 * B, D), preferred_element_type=jnp.float32)
-    for n in range(9):
-        part[n] = slices[:, n * B : (n + 1) * B].astype(jnp.bfloat16)
-
     def rs_copy(n, to):
         return copy(part.at[n], sums.at[b], rs_s.at[n], rs_r.at[b], of_column(to))
 
-    for n, to in enumerate(OWNER):
-        @pl.when(b != to)
-        def _():
-            rs_copy(n, to).start()
-
-        @pl.when(b == to)
-        def _():
-            sums[b] = part[n]
+    for first in range(0, 9, 2):
+        blocks = range(first, min(first + 2, 9))
+        columns = feats[:, :, :, :, first * B : blocks.stop * B].reshape(16 * B, len(blocks) * B)
+        slices = jnp.dot(gp_in[...], columns, preferred_element_type=jnp.float32)
+        for n in blocks:
+            part[n] = slices[:, (n - first) * B : (n - first + 1) * B].astype(jnp.bfloat16)
+
+            @pl.when(b != OWNER[n])
+            def _():
+                rs_copy(n, OWNER[n]).start()
+
+            @pl.when(b == OWNER[n])
+            def _():
+                sums[b] = part[n]
 
     process_texts(1)
     band_forward(1, txts, 2)

time: 102 us -> 101 us (level); the launches traced: 102 us -> 100 us
  Pallas kernels: 102 us -> 99.4 us
    pallas_call x1, Pallas kernels: 96.1 us -> 93.9 us  [shards(): pl.pallas_call(kernel, out_shape=(jax.ShapeDtypeStruct((B, D), bf), jax.S...]
where the time goes in v5:
time: 101 us; the launch traced here: 100 us
  Pallas kernels  99.4 us (98%)
    pallas_call x1, Pallas kernels, shards(): pl.pallas_call(kernel, out_shape=(jax.ShapeDtypeStruct((B, D), bf), jax.S...  93.9 us
    pallas_call x1, Pallas kernels, shards(): pl.pallas_call(finish, grid=(D // WIDE,), out_shape=(jax.ShapeDtypeStruct...  5.53 us

profile of v5, /device:TPU:1, one launch (start us, length us, event | category | flops | bytes accessed | tf_op | source)
XLA Modules:
  0.0 100.0 jit_solution(9032066072982441101)
XLA Ops:
  0.6 93.9 %shard_map.76 = (bf16[128,1152]{1,0:T(8,128)(2,1)}, bf16[128,1152]{1,0:T(8,128)(2,1)}, bf16[4,2,2,80,1152]{4,3,2,1,0:T(8,128)(2,1)}) custom-call(bf16[128,1152]{1,0:T(8,128)(2,1)} %img_hbm.1, s32[1,128]{1,0:T(1,128)} %bitcast.2, bf16[128,1152]{1,0:T(8,128)(2,1)} %txt_hbm.1, s32[1,128]{1,0:T(1,128)} %bitcast.3, bf16[1152,1152]{1,0:T(8,128)(2,1)} %head_hbm.1), custom_call_target="tpu_custom_call" | custom-call | tf_op jit(solution)/shard_map/pallas_call | solution.py:642
  94.5 5.5 %shard_map.77 = (bf16[128,1152]{1,0:T(8,128)(2,1)}, bf16[128,1152]{1,0:T(8,128)(2,1)}, f32[1152,1152]{1,0:T(8,128)}) custom-call(bf16[4,2,2,80,1152]{4,3,2,1,0:T(8,128)(2,1)} %get-tuple-element.6.g_ref, bf16[128,1152]{1,0:T(8,128)(2,1)} %get-tuple-element.7.gimg_ref, bf16[128,1152]{1,0:T(8,128)(2,1)} %get-tuple-element.8.gtxt_ref), custom_call_target="tpu_custom_call" | custom-call | tf_op jit(solution)/shard_map/pallas_call | solution.py:657

commit v6 on v5

--- a/solution.py
+++ b/solution.py
@@ -367,6 +367,7 @@
     gtxt_ref[...] = lax.dot_general(
         grad_pre, head_ref[...], NT, preferred_element_type=jnp.float32
     ).astype(jnp.bfloat16)
+    process_texts(1)
     feats_wait()
 
     def gp_wait(i, carry):
@@ -392,7 +393,6 @@
             def _():
                 sums[b] = part[n]
 
-    process_texts(1)
     band_forward(1, txts, 2)
     mine = jnp.where(g == 0, jnp.where(b == 2, 4, z // 2), 5 + z // 2)
     is_owner = jnp.logical_or(lax.rem(z, 2) == g, b == 2)
@@ -490,7 +490,6 @@
             def _():
                 second_x(i, gg).start()
         second_y(i).start()
-    process_texts(2)
     for i in ORDER:
         for gg in range(2):
             @pl.when(back(x, i) // 2 == gg)
@@ -508,6 +507,7 @@
     keep_y(0).start()
 
 
+    process_texts(2)
     band_wait(1, txts, 3)
     process_texts(3)
     swap_i = send(acc_i.at[pl.ds(B, B)], got_i, pair_s.at[3], pair_r.at[3], mate)

time: 101 us -> 100 us (0.990)
  no operation moved by 1% of the time
where the time goes in v6:
time: 100 us
  Pallas kernels  99.4 us (99%)
    pallas_call x1, Pallas kernels, shards(): pl.pallas_call(kernel, out_shape=(jax.ShapeDtypeStruct((B, D), bf), jax.S...  93.9 us
    pallas_call x1, Pallas kernels, shards(): pl.pallas_call(finish, grid=(D // WIDE,), out_shape=(jax.ShapeDtypeStruct...  5.53 us

profile of v6, /device:TPU:1, one launch (start us, length us, event | category | flops | bytes accessed | tf_op | source)
XLA Modules:
  0.0 100.0 jit_solution(9950797179785072050)
XLA Ops:
  0.6 93.9 %shard_map.76 = (bf16[128,1152]{1,0:T(8,128)(2,1)}, bf16[128,1152]{1,0:T(8,128)(2,1)}, bf16[4,2,2,80,1152]{4,3,2,1,0:T(8,128)(2,1)}) custom-call(bf16[128,1152]{1,0:T(8,128)(2,1)} %img_hbm.1, s32[1,128]{1,0:T(1,128)} %bitcast.2, bf16[128,1152]{1,0:T(8,128)(2,1)} %txt_hbm.1, s32[1,128]{1,0:T(1,128)} %bitcast.3, bf16[1152,1152]{1,0:T(8,128)(2,1)} %head_hbm.1), custom_call_target="tpu_custom_call" | custom-call | tf_op jit(solution)/shard_map/pallas_call | solution.py:642
  94.5 5.5 %shard_map.77 = (bf16[128,1152]{1,0:T(8,128)(2,1)}, bf16[128,1152]{1,0:T(8,128)(2,1)}, f32[1152,1152]{1,0:T(8,128)}) custom-call(bf16[4,2,2,80,1152]{4,3,2,1,0:T(8,128)(2,1)} %get-tuple-element.6.g_ref, bf16[128,1152]{1,0:T(8,128)(2,1)} %get-tuple-element.7.gimg_ref, bf16[128,1152]{1,0:T(8,128)(2,1)} %get-tuple-element.8.gtxt_ref), custom_call_target="tpu_custom_call" | custom-call | tf_op jit(solution)/shard_map/pallas_call | solution.py:657

commit v7 on v6

--- a/solution.py
+++ b/solution.py
@@ -364,9 +364,6 @@
     gp_in[:, pl.ds(pl.multiple_of(a * B, B), B)] = gp_t[pl.ds(start_row(a), SLICE)]
     band_forward(1, txts, 1)
     feats_fourth()
-    gtxt_ref[...] = lax.dot_general(
-        grad_pre, head_ref[...], NT, preferred_element_type=jnp.float32
-    ).astype(jnp.bfloat16)
     process_texts(1)
     feats_wait()
 
@@ -418,11 +415,8 @@
         block[...] = total.astype(jnp.bfloat16)
         g_vm[y, xp, core, :, lanes] = total.astype(jnp.bfloat16)
 
-        def az_send(i, carry):
+        for i in (4, 5, 3, 6, 2, 7, 1):
             az_copy(i).start()
-            return carry
-
-        lax.fori_loop(1, 8, az_send, 0)
 
     for gg, (first, count) in enumerate(((0, 5), (5, 4))):
         for n in range(first, first + count):
@@ -507,6 +501,9 @@
     keep_y(0).start()
 
 
+    gtxt_ref[...] = lax.dot_general(
+        grad_pre, head_ref[...], NT, preferred_element_type=jnp.float32
+    ).astype(jnp.bfloat16)
     process_texts(2)
     band_wait(1, txts, 3)
     process_texts(3)

time: 100 us -> 101 us (1.010)
  no operation moved by 1% of the time
where the time goes in v7:
time: 101 us; the launch traced here: 100 us
  Pallas kernels  99.8 us (99%)
    pallas_call x1, Pallas kernels, shards(): pl.pallas_call(kernel, out_shape=(jax.ShapeDtypeStruct((B, D), bf), jax.S...  94.3 us
    pallas_call x1, Pallas kernels, shards(): pl.pallas_call(finish, grid=(D // WIDE,), out_shape=(jax.ShapeDtypeStruct...  5.52 us

profile of v7, /device:TPU:1, one launch (start us, length us, event | category | flops | bytes accessed | tf_op | source)
XLA Modules:
  0.0 100.4 jit_solution(4230944954728050962)
XLA Ops:
  0.6 94.3 %shard_map.76 = (bf16[128,1152]{1,0:T(8,128)(2,1)}, bf16[128,1152]{1,0:T(8,128)(2,1)}, bf16[4,2,2,80,1152]{4,3,2,1,0:T(8,128)(2,1)}) custom-call(bf16[128,1152]{1,0:T(8,128)(2,1)} %img_hbm.1, s32[1,128]{1,0:T(1,128)} %bitcast.2, bf16[128,1152]{1,0:T(8,128)(2,1)} %txt_hbm.1, s32[1,128]{1,0:T(1,128)} %bitcast.3, bf16[1152,1152]{1,0:T(8,128)(2,1)} %head_hbm.1), custom_call_target="tpu_custom_call" | custom-call | tf_op jit(solution)/shard_map/pallas_call | solution.py:639
  94.9 5.5 %shard_map.77 = (bf16[128,1152]{1,0:T(8,128)(2,1)}, bf16[128,1152]{1,0:T(8,128)(2,1)}, f32[1152,1152]{1,0:T(8,128)}) custom-call(bf16[4,2,2,80,1152]{4,3,2,1,0:T(8,128)(2,1)} %get-tuple-element.6.g_ref, bf16[128,1152]{1,0:T(8,128)(2,1)} %get-tuple-element.7.gimg_ref, bf16[128,1152]{1,0:T(8,128)(2,1)} %get-tuple-element.8.gtxt_ref), custom_call_target="tpu_custom_call" | custom-call | tf_op jit(solution)/shard_map/pallas_call | solution.py:654
